TPU v7x, 256 devices: a whole 4x4x8 slice. The times are simulated.
256 devices in a mesh: blk: 4 (over y), branch: 64 (over z, x, core).
Axes of the slice: x: 4, y: 4, z: 8, core: 2. Of those that a mesh axis runs over, the one named last changes fastest.
Arguments:
- queries: bfloat16 [128, 32, 8192], P('branch', None, 'blk'), may hold values from -400 to 400
- root_kv: bfloat16 [4096, 2, 1024], P('branch', None, 'blk'), may hold values from -6 to 6
- node_kv: bfloat16 [192, 128, 2, 1024], P('branch', None, None, 'blk'), may hold values from -6 to 6
- own_kv: bfloat16 [128, 32, 2, 1024], P('branch', None, None, 'blk'), may hold values from -6 to 6
- anc_owner: int32 [128, 8], P('branch'), may hold values from 0 to 63, all different within a row; in each aligned block of 2 rows (0 to 1, 2 to 3, ...) at most 2 rows name the same one
- anc_slot: int32 [128, 8], P('branch'), may hold values from 0 to 2
- depth_len: int32 [128], P('branch'), may hold values from 1 to 8
- seg_len: int32 [128], P('branch'), may hold values from 1 to 32
- norm_gain: bfloat16 [8192], P('blk'), may hold values from 0.099609375 to 1.8984375
Outputs:
- normed: bfloat16 [128, 32, 8192], P('branch', None, 'blk')
Inputs may be any that keep to these rules, and one draw needn't show every extreme that they name: `anc_owner`: each branch's row names 8 different owners; among the 2 rows of one index of branch, no owner is named more than 2 times, a bound that some block reaches.
All inputs are finite; a program needn't handle non-finite values.
Results may differ from a plain program's by a relative error of at most 0.008.
Values may be sent and summed in bfloat16 or wider, within the bound.
A program may use at most 128 MiB of HBM per device.

v0:
```python
import math

import jax
import jax.numpy as jnp
from jax import lax
from jax.sharding import PartitionSpec as P

HEADS = 64
HEAD_DIM = 128


def absorb(carry, scores, values, seen, form):
    top, total, acc = carry
    scores = jnp.where(seen, scores, -1e30)
    new_top = jnp.maximum(top, jnp.max(scores, axis=-1))
    factor = jnp.exp(top - new_top)
    weights = jnp.where(seen, jnp.exp(scores - new_top[..., None]), 0.0)
    total = total * factor + jnp.sum(weights, axis=-1)
    update = jnp.einsum(
        form, weights.astype(jnp.bfloat16), values, preferred_element_type=jnp.float32
    )
    acc = acc * factor[..., None] + update
    return (new_top, total, acc)


def on_device(
    queries, root_kv, node_kv, own_kv, anc_owner, anc_slot, depth_len, seg_len, norm_gain
):
    branches, seg, qwidth = queries.shape
    kwidth = root_kv.shape[2]
    kv_local = kwidth // HEAD_DIM
    group = qwidth // kwidth
    depth = anc_owner.shape[1]
    block = node_kv.shape[1]
    held = node_kv.shape[0]
    scale = 1.0 / math.sqrt(HEAD_DIM)
    heads = queries.reshape(branches, seg, kv_local, group, HEAD_DIM)
    start_state = (
        jnp.full((branches, seg, kv_local, group), -1e30, jnp.float32),
        jnp.zeros((branches, seg, kv_local, group), jnp.float32),
        jnp.zeros((branches, seg, kv_local, group, HEAD_DIM), jnp.float32),
    )
    piece = lax.all_gather(root_kv, "branch", axis=0, tiled=True)
    fold_keys = piece[:, 0].reshape(piece.shape[0], kv_local, HEAD_DIM)
    fold_values = piece[:, 1].reshape(piece.shape[0], kv_local, HEAD_DIM)
    fold_scores = (
        jnp.einsum("bskgd,nkd->bskgn", heads, fold_keys, preferred_element_type=jnp.float32) * scale
    )
    state = absorb(start_state, fold_scores, fold_values, True, "bskgn,nkd->bskgd")
    node_ids = (anc_owner * held + anc_slot).reshape(branches * depth)
    gathered = lax.all_gather(node_kv, "branch", axis=0, tiled=True)
    ancestors = gathered[node_ids].reshape(branches, depth, block, 2, kwidth)
    for level in range(depth):
        level_blocks = ancestors[:, level]
        keys = level_blocks[:, :, 0].reshape(branches, block, kv_local, HEAD_DIM)
        values = level_blocks[:, :, 1].reshape(branches, block, kv_local, HEAD_DIM)
        scores = (
            jnp.einsum("bskgd,bnkd->bskgn", heads, keys, preferred_element_type=jnp.float32) * scale
        )
        visible = (level < depth_len)[:, None, None, None, None]
        state = absorb(state, scores, values, visible, "bskgn,bnkd->bskgd")
    own_keys = own_kv[:, :, 0].reshape(branches, seg, kv_local, HEAD_DIM)
    own_values = own_kv[:, :, 1].reshape(branches, seg, kv_local, HEAD_DIM)
    scores = (
        jnp.einsum("bskgd,bnkd->bskgn", heads, own_keys, preferred_element_type=jnp.float32) * scale
    )
    positions = jnp.arange(seg)
    causal = (positions[None, :] <= positions[:, None])[None, :, None, None, :]
    state = absorb(state, scores, own_values, causal, "bskgn,bnkd->bskgd")
    top, total, acc = state
    attended = (acc / total[..., None]).reshape(branches, seg, qwidth)
    live = positions[None, :] < seg_len[:, None]
    attended = jnp.where(live[:, :, None], attended, 0.0)
    squares = lax.psum(jnp.sum(attended * attended, axis=-1), "blk")
    inverse = lax.rsqrt(squares / (HEADS * HEAD_DIM) + 1e-06)
    result = attended * inverse[:, :, None] * norm_gain.astype(jnp.float32)[None, None, :]
    return result.astype(jnp.bfloat16)


def solution(mesh):
    in_specs = (
        P("branch", None, "blk"),
        P("branch", None, "blk"),
        P("branch", None, None, "blk"),
        P("branch", None, None, "blk"),
        P("branch", None),
        P("branch", None),
        P("branch"),
        P("branch"),
        P("blk"),
    )
    out_specs = P("branch", None, "blk")
    return jax.shard_map(
        on_device, mesh=mesh, in_specs=in_specs, out_specs=out_specs, check_vma=False
    )
```

profile of v0, /device:TPU:2, one launch (start us, length us, event | category | flops | bytes accessed | tf_op | source)
XLA Modules:
  0.0 300.5 jit_solution(8707701948924970989)
XLA Ops:
  6.5 0.7 all-gather.3.cloned.1.call-update
  7.3 1.8 copy.364
  9.1 0.7 multiply_add_fusion
  9.9 1.0 copy.509
  10.9 1.2 slice_reduce_fusion
  12.8 1.3 convert_element_type.46
  14.1 1.3 iota_compare_fusion.1
  15.4 1.2 broadcast_compare_fusion.7
  16.7 1.9 fusion.151
  18.6 72.4 %all-gather.3.cloned.1.call-done = bf16[4096,2,256]{2,1,0:T(2,128)(2,1)} async-done(((bf16[64,2,256]{2,1,0:T(2,128)(2,1)}), bf16[4096,2,256]{2,1,0:T(2,128)(2,1)}) %all-gather.3.cloned.1.call-update) | async-done | bytes 4194320 | tf_op jit(solution)/shard_map/all_gather | solution.py:43
  91.0 9.9 %fusion.142 = (bf16[4096,1,256]{2,1,0:T(2,128)(2,1)}, bf16[4096,1,256]{2,1,0:T(2,128)(2,1)}) fusion(bf16[4096,2,256]{2,1,0:T(2,128)(2,1)} %all-gather.3.cloned.1.call-done), kind=kLoop, calls=%fused_computation.195 | loop fusion | bytes 8388608 | tf_op jit(solution)/shard_map/slice | solution.py:45
  100.9 8.6 %copy.507 = bf16[4096,1,256]{0,2,1:T(8,128)(2,1)S(1)} copy(bf16[4096,1,256]{2,1,0:T(2,128)(2,1)} %get-tuple-element.27) | data formatting | bytes 4194304
  109.5 9.7 %copy.508 = bf16[4096,1,256]{0,2,1:T(8,128)(2,1)} copy(bf16[4096,1,256]{2,1,0:T(2,128)(2,1)} %get-tuple-element.26) | data formatting | bytes 4194304
  119.3 8.6 %bitcast_reduce_fusion = (f32[2,32,2,8]{1,3,0,2:T(8,128)}, f32[2,4096,2,32,8]{1,3,4,2,0:T(8,128)}) fusion(bf16[4096,2,128,1,1]{0,2,4,3,1:T(8,128)(2,1)S(1)} %bitcast.193, bf16[2,32,2,8,128]{4,3,2,1,0:T(8,128)(2,1)S(1)} %bitcast.184), kind=kOutput, calls=%fused_computation.2 | convolution fusion | flops 1082129408 | bytes 19140608 | tf_op jit(solution)/shard_map/bskgd,nkd->bskgn/dot_general | solution.py:47
  127.9 84.3 %all-gather.5.cloned.1.call-done = bf16[192,128,2,256]{3,1,2,0:T(8,128)(2,1)} async-done(((bf16[3,128,2,256]{3,1,2,0:T(8,128)(2,1)}), bf16[192,128,2,256]{3,1,2,0:T(8,128)(2,1)}) %all-gather.5.cloned.1.call-update) | async-done | bytes 25165840 | tf_op jit(solution)/shard_map/all_gather | solution.py:51
  212.2 8.8 %gather_fusion = bf16[16,128,2,256]{3,1,2,0:T(8,128)(2,1)S(1)} fusion(bf16[192,128,2,256]{3,1,2,0:T(8,128)(2,1)} %all-gather.5.cloned.1.call-done, s32[1024]{0:T(1024)S(1)} %pad_clamp_fusion), kind=kCustom, calls=%fused_computation | custom fusion | bytes 4194368 | tf_op jit(solution)/shard_map/gather | solution.py:52
  221.0 1.0 slice_bitcast_fusion.7
  222.0 0.7 fusion.145
  223.0 1.9 fusion.147
  225.1 0.7 fusion.143
  226.0 0.7 fusion.149
  227.2 1.6 fusion.157
  228.8 1.0 fusion.158
  229.8 1.7 fusion.156
  231.5 1.0 fusion.155
  234.1 1.4 copy_maximum_fusion
  235.6 1.6 fusion.52
  237.2 1.8 convolution_bitcast_fusion.7
  239.0 1.0 copy.381
  240.0 2.0 fusion.54
  242.1 2.2 convolution_bitcast_fusion.6
  244.3 1.0 copy.387
  245.3 2.0 fusion.56
  247.3 2.2 convolution_bitcast_fusion.5
  249.6 1.0 fusion.58
  250.6 1.1 convolution_bitcast_fusion.4
  251.7 1.0 copy.399
  253.2 1.2 convolution_bitcast_fusion.3
  254.3 1.0 copy.369
  255.4 1.0 copy.411
  257.5 9.0 %fusion.1 = f32[2,32,2,8]{1,3,0,2:T(8,128)S(1)} fusion(f32[2,4096,2,32,8]{1,3,4,2,0:T(8,128)} %get-tuple-element.83, f32[2,32,2,8]{1,3,0,2:T(8,128)} %get-tuple-element.55), kind=kLoop, calls=%fused_computation.4 | loop fusion | flops 12581888 | bytes 16785408 | tf_op jit(solution)/shard_map/reduce_sum | solution.py:18
  267.4 0.9 fusion.67
  268.3 0.7 copy_add_fusion
  269.2 7.6 %fusion.47 = f32[2,32,2,8,128]{4,1,3,0,2:T(8,128)S(1)} fusion(bf16[4096,2,128,1,1]{0,2,4,3,1:T(8,128)(2,1)S(1)} %bitcast.195, f32[2,4096,2,32,8]{1,3,4,2,0:T(8,128)} %get-tuple-element.83, f32[2,32,2,8]{1,3,0,2:T(8,128)} %get-tuple-element.55, f32[2,32,2,8]{1,3,0,2:T(8,128)} %get-tuple-element.16, f32[2,32,2,8]{1,3,0,2:T(8,128)} %get-tuple-element.54), kind=kOutput, calls=%fused_computation.63 | convolution fusion | flops 1086586880 | bytes 19410944 | tf_op jit(solution)/shard_map/bskgn,nkd->bskgd/dot_general | solution.py:19
  276.9 2.2 fusion.39
  279.8 1.4 multiply_reduce_fusion
  281.6 10.5 %psum.7 = f32[2,32]{1,0:T(2,128)S(1)} all-reduce(f32[2,32]{1,0:T(2,128)S(1)} %get-tuple-element.84), channel_id=1, replica_groups=mesh['blk'=4,'branch'=64] {'blk'}, use_global_device_ids=true, to_apply=%region_21.22 | all-reduce | flops 64 | bytes 512 | tf_op jit(solution)/shard_map/psum | solution.py:74
  292.1 1.6 multiply_convert_fusion
  (129 shorter events, 6.8 us)
Async XLA Ops:
  6.5 84.4 %all-gather.3.cloned.1.call-start = ((), (), s32[]{:S(2)}) async-start(), calls=%async_computation | async-start | bytes 4259840 | tf_op jit(solution)/shard_map/all_gather | solution.py:43
  7.3 204.9 %all-gather.5.cloned.1.call-start = ((), (), s32[]{:S(2)}) async-start(), calls=%async_computation.1 | async-start | bytes 25559040 | tf_op jit(solution)/shard_map/all_gather | solution.py:51
  16.6 215.9 %copy-start.39 = (pred[2]{0:T(512)(128)(4,1)}, pred[2]{0:T(512)(128)(4,1)S(1)}, u32[]{:S(2)}) copy-start(pred[2]{0:T(512)(128)(4,1)S(1)} %get-tuple-element.56) | copy-start | bytes 10
  16.6 216.3 %copy-start.37 = (pred[2]{0:T(512)(128)(4,1)}, pred[2]{0:T(512)(128)(4,1)S(1)}, u32[]{:S(2)}) copy-start(pred[2]{0:T(512)(128)(4,1)S(1)} %get-tuple-element.63) | copy-start | bytes 10
  16.6 216.7 %copy-start.44 = (pred[2]{0:T(512)(128)(4,1)}, pred[2]{0:T(512)(128)(4,1)S(1)}, u32[]{:S(2)}) copy-start(pred[2]{0:T(512)(128)(4,1)S(1)} %get-tuple-element.57) | copy-start | bytes 10
  16.6 217.1 %copy-start.42 = (pred[2]{0:T(512)(128)(4,1)}, pred[2]{0:T(512)(128)(4,1)S(1)}, u32[]{:S(2)}) copy-start(pred[2]{0:T(512)(128)(4,1)S(1)} %get-tuple-element.62) | copy-start | bytes 10
  225.7 23.7 %copy-start.6 = (bf16[2,128,1,256]{3,1,2,0:T(8,128)(2,1)S(1)}, bf16[2,128,1,256]{3,1,2,0:T(8,128)(2,1)}, u32[]{:S(2)}) copy-start(bf16[2,128,1,256]{3,1,2,0:T(8,128)(2,1)} %get-tuple-element.91) | copy-start | bytes 393220
  225.8 23.9 %copy-start.46 = (pred[2]{0:T(512)(128)(4,1)S(1)}, pred[2]{0:T(512)(128)(4,1)}, u32[]{:S(2)}) copy-start(pred[2]{0:T(512)(128)(4,1)} %get-tuple-element.58) | copy-start | bytes 10
  233.7 19.0 %copy-start.45 = (pred[2]{0:T(512)(128)(4,1)S(1)}, pred[2]{0:T(512)(128)(4,1)}, u32[]{:S(2)}) copy-start(pred[2]{0:T(512)(128)(4,1)} %copy-done.44) | copy-start | bytes 10
  234.1 22.3 %copy-start.43 = (pred[2]{0:T(512)(128)(4,1)S(1)}, pred[2]{0:T(512)(128)(4,1)}, u32[]{:S(2)}) copy-start(pred[2]{0:T(512)(128)(4,1)} %copy-done.42) | copy-start | bytes 10
  235.5 21.8 %copy-start.8 = (f32[2,32,2,8]{1,3,0,2:T(8,128)}, f32[2,32,2,8]{1,3,0,2:T(8,128)S(1)}, u32[]{:S(2)}) copy-start(f32[2,32,2,8]{1,3,0,2:T(8,128)S(1)} %get-tuple-element.18) | copy-start | bytes 12292
  235.5 21.8 %copy-start.10 = (f32[2,32,2,8]{1,3,0,2:T(8,128)}, f32[2,32,2,8]{1,3,0,2:T(8,128)S(1)}, u32[]{:S(2)}) copy-start(f32[2,32,2,8]{1,3,0,2:T(8,128)S(1)} %get-tuple-element.20) | copy-start | bytes 12292
  235.5 21.8 %copy-start.12 = (f32[2,32,2,8]{1,3,0,2:T(8,128)}, f32[2,32,2,8]{1,3,0,2:T(8,128)S(1)}, u32[]{:S(2)}) copy-start(f32[2,32,2,8]{1,3,0,2:T(8,128)S(1)} %get-tuple-element.21) | copy-start | bytes 12292
  235.5 21.8 %copy-start.14 = (f32[2,32,2,8]{1,3,0,2:T(8,128)}, f32[2,32,2,8]{1,3,0,2:T(8,128)S(1)}, u32[]{:S(2)}) copy-start(f32[2,32,2,8]{1,3,0,2:T(8,128)S(1)} %get-tuple-element.22) | copy-start | bytes 12292
  235.5 21.8 %copy-start.16 = (f32[2,32,2,8]{1,3,0,2:T(8,128)}, f32[2,32,2,8]{1,3,0,2:T(8,128)S(1)}, u32[]{:S(2)}) copy-start(f32[2,32,2,8]{1,3,0,2:T(8,128)S(1)} %get-tuple-element.23) | copy-start | bytes 12292
  235.6 21.8 %copy-start.18 = (f32[2,32,2,8]{1,3,0,2:T(8,128)}, f32[2,32,2,8]{1,3,0,2:T(8,128)S(1)}, u32[]{:S(2)}) copy-start(f32[2,32,2,8]{1,3,0,2:T(8,128)S(1)} %get-tuple-element.24) | copy-start | bytes 12292
  257.3 9.2 %copy-start.7 = (f32[2,32,2,8]{1,3,0,2:T(8,128)S(1)}, f32[2,32,2,8]{1,3,0,2:T(8,128)}, u32[]{:S(2)}) copy-start(f32[2,32,2,8]{1,3,0,2:T(8,128)} %get-tuple-element.25) | copy-start | bytes 12292
  257.4 9.2 %copy-start.40 = (pred[2]{0:T(512)(128)(4,1)S(1)}, pred[2]{0:T(512)(128)(4,1)}, u32[]{:S(2)}) copy-start(pred[2]{0:T(512)(128)(4,1)} %copy-done.39) | copy-start | bytes 10
  257.4 9.6 %copy-start.38 = (pred[2]{0:T(512)(128)(4,1)S(1)}, pred[2]{0:T(512)(128)(4,1)}, u32[]{:S(2)}) copy-start(pred[2]{0:T(512)(128)(4,1)} %copy-done.37) | copy-start | bytes 10
  257.4 10.0 %copy-start.5 = (f32[2,32,2,8,32]{1,4,3,2,0:T(8,128)S(1)}, f32[2,32,2,8,32]{1,4,3,2,0:T(8,128)}, u32[]{:S(2)}) copy-start(f32[2,32,2,8,32]{1,4,3,2,0:T(8,128)} %get-tuple-element.65) | copy-start | bytes 393220
  257.4 10.0 %copy-start.33 = (f32[2,32,2,8]{1,3,0,2:T(8,128)S(1)}, f32[2,32,2,8]{1,3,0,2:T(8,128)}, u32[]{:S(2)}) copy-start(f32[2,32,2,8]{1,3,0,2:T(8,128)} %get-tuple-element.17) | copy-start | bytes 12292
  257.4 10.0 %copy-start.35 = (pred[32,32]{0,1:T(8,128)(4,1)S(1)}, pred[32,32]{0,1:T(8,128)(4,1)}, u32[]{:S(2)}) copy-start(pred[32,32]{0,1:T(8,128)(4,1)} %copy-done.34) | copy-start | bytes 3076
  257.4 10.8 %copy-start.9 = (f32[2,32,2,8]{1,3,0,2:T(8,128)S(1)}, f32[2,32,2,8]{1,3,0,2:T(8,128)}, u32[]{:S(2)}) copy-start(f32[2,32,2,8]{1,3,0,2:T(8,128)} %copy-done.8) | copy-start | bytes 12292
  257.4 10.8 %copy-start.11 = (f32[2,32,2,8]{1,3,0,2:T(8,128)S(1)}, f32[2,32,2,8]{1,3,0,2:T(8,128)}, u32[]{:S(2)}) copy-start(f32[2,32,2,8]{1,3,0,2:T(8,128)} %copy-done.10) | copy-start | bytes 12292
  257.4 10.8 %copy-start.13 = (f32[2,32,2,8]{1,3,0,2:T(8,128)S(1)}, f32[2,32,2,8]{1,3,0,2:T(8,128)}, u32[]{:S(2)}) copy-start(f32[2,32,2,8]{1,3,0,2:T(8,128)} %copy-done.12) | copy-start | bytes 12292
  257.4 10.8 %copy-start.15 = (f32[2,32,2,8]{1,3,0,2:T(8,128)S(1)}, f32[2,32,2,8]{1,3,0,2:T(8,128)}, u32[]{:S(2)}) copy-start(f32[2,32,2,8]{1,3,0,2:T(8,128)} %copy-done.14) | copy-start | bytes 12292
  257.4 10.8 %copy-start.17 = (f32[2,32,2,8]{1,3,0,2:T(8,128)S(1)}, f32[2,32,2,8]{1,3,0,2:T(8,128)}, u32[]{:S(2)}) copy-start(f32[2,32,2,8]{1,3,0,2:T(8,128)} %copy-done.16) | copy-start | bytes 12292
  257.5 10.8 %copy-start.19 = (f32[2,32,2,8]{1,3,0,2:T(8,128)S(1)}, f32[2,32,2,8]{1,3,0,2:T(8,128)}, u32[]{:S(2)}) copy-start(f32[2,32,2,8]{1,3,0,2:T(8,128)} %copy-done.18) | copy-start | bytes 12292
  257.5 10.8 %copy-start.20 = (f32[2,32,2,8]{1,3,0,2:T(8,128)S(1)}, f32[2,32,2,8]{1,3,0,2:T(8,128)}, u32[]{:S(2)}) copy-start(f32[2,32,2,8]{1,3,0,2:T(8,128)} %get-tuple-element.82) | copy-start | bytes 12292
  257.5 10.8 %copy-start.21 = (f32[2,32,2,8]{1,3,2,0:T(8,128)S(1)}, f32[2,32,2,8]{1,3,2,0:T(8,128)}, u32[]{:S(2)}) copy-start(f32[2,32,2,8]{1,3,2,0:T(8,128)} %get-tuple-element.64) | copy-start | bytes 12292
  257.5 10.8 %copy-start.29 = (f32[2,32,2,8]{1,3,0,2:T(8,128)S(1)}, f32[2,32,2,8]{1,3,0,2:T(8,128)}, u32[]{:S(2)}) copy-start(f32[2,32,2,8]{1,3,0,2:T(8,128)} %fusion.52) | copy-start | bytes 12292
  257.5 10.8 %copy-start.30 = (f32[2,32,2,8]{1,3,0,2:T(8,128)S(1)}, f32[2,32,2,8]{1,3,0,2:T(8,128)}, u32[]{:S(2)}) copy-start(f32[2,32,2,8]{1,3,0,2:T(8,128)} %fusion.54) | copy-start | bytes 12292
  257.5 10.8 %copy-start.31 = (f32[2,32,2,8]{1,3,0,2:T(8,128)S(1)}, f32[2,32,2,8]{1,3,0,2:T(8,128)}, u32[]{:S(2)}) copy-start(f32[2,32,2,8]{1,3,0,2:T(8,128)} %fusion.56) | copy-start | bytes 12292
  257.5 10.8 %copy-start.32 = (f32[2,32,2,8]{1,3,0,2:T(8,128)S(1)}, f32[2,32,2,8]{1,3,0,2:T(8,128)}, u32[]{:S(2)}) copy-start(f32[2,32,2,8]{1,3,0,2:T(8,128)} %fusion.58) | copy-start | bytes 12292
  257.5 11.5 %copy-start = (bf16[4096,1,256]{0,2,1:T(8,128)(2,1)S(1)}, bf16[4096,1,256]{0,2,1:T(8,128)(2,1)}, u32[]{:S(2)}) copy-start(bf16[4096,1,256]{0,2,1:T(8,128)(2,1)} %copy.508) | copy-start | bytes 6291460
  269.0 7.8 %copy-start.1 = (f32[2,32,2,8,128]{4,1,3,0,2:T(8,128)S(1)}, f32[2,32,2,8,128]{4,1,3,0,2:T(8,128)}, u32[]{:S(2)}) copy-start(f32[2,32,2,8,128]{4,1,3,0,2:T(8,128)} %convolution_bitcast_fusion.7) | copy-start | bytes 1572868
  269.0 7.8 %copy-start.2 = (f32[2,32,2,8,128]{4,1,3,0,2:T(8,128)S(1)}, f32[2,32,2,8,128]{4,1,3,0,2:T(8,128)}, u32[]{:S(2)}) copy-start(f32[2,32,2,8,128]{4,1,3,0,2:T(8,128)} %convolution_bitcast_fusion.6) | copy-start | bytes 1572868
  269.1 7.8 %copy-start.3 = (f32[2,32,2,8,128]{4,1,3,0,2:T(8,128)S(1)}, f32[2,32,2,8,128]{4,1,3,0,2:T(8,128)}, u32[]{:S(2)}) copy-start(f32[2,32,2,8,128]{4,1,3,0,2:T(8,128)} %convolution_bitcast_fusion.5) | copy-start | bytes 1572868
  269.1 7.8 %copy-start.4 = (f32[2,32,2,8,128]{4,1,3,0,2:T(8,128)S(1)}, f32[2,32,2,8,128]{4,1,3,0,2:T(8,128)}, u32[]{:S(2)}) copy-start(f32[2,32,2,8,128]{4,1,3,0,2:T(8,128)} %convolution_bitcast_fusion.4) | copy-start | bytes 1572868
  269.1 7.8 %copy-start.24 = (f32[2,32,2,8]{1,3,0,2:T(8,128)S(1)}, f32[2,32,2,8]{1,3,0,2:T(8,128)}, u32[]{:S(2)}) copy-start(f32[2,32,2,8]{1,3,0,2:T(8,128)} %get-tuple-element.10) | copy-start | bytes 12292
  269.1 7.8 %copy-start.25 = (f32[2,32,2,8]{1,3,0,2:T(8,128)S(1)}, f32[2,32,2,8]{1,3,0,2:T(8,128)}, u32[]{:S(2)}) copy-start(f32[2,32,2,8]{1,3,0,2:T(8,128)} %get-tuple-element.11) | copy-start | bytes 12292
  269.1 7.8 %copy-start.26 = (f32[2,32,2,8]{1,3,0,2:T(8,128)S(1)}, f32[2,32,2,8]{1,3,0,2:T(8,128)}, u32[]{:S(2)}) copy-start(f32[2,32,2,8]{1,3,0,2:T(8,128)} %get-tuple-element.12) | copy-start | bytes 12292
  269.1 7.8 %copy-start.27 = (f32[2,32,2,8]{1,3,0,2:T(8,128)S(1)}, f32[2,32,2,8]{1,3,0,2:T(8,128)}, u32[]{:S(2)}) copy-start(f32[2,32,2,8]{1,3,0,2:T(8,128)} %get-tuple-element.13) | copy-start | bytes 12292
  269.1 7.8 %copy-start.28 = (f32[2,32,2,8]{1,3,0,2:T(8,128)S(1)}, f32[2,32,2,8]{1,3,0,2:T(8,128)}, u32[]{:S(2)}) copy-start(f32[2,32,2,8]{1,3,0,2:T(8,128)} %get-tuple-element.14) | copy-start | bytes 12292
  269.1 10.0 %copy-start.22 = (f32[2,32,2,8]{1,3,0,2:T(8,128)S(1)}, f32[2,32,2,8]{1,3,0,2:T(8,128)}, u32[]{:S(2)}) copy-start(f32[2,32,2,8]{1,3,0,2:T(8,128)} %get-tuple-element.8) | copy-start | bytes 12292
  269.1 10.0 %copy-start.23 = (f32[2,32,2,8]{1,3,0,2:T(8,128)S(1)}, f32[2,32,2,8]{1,3,0,2:T(8,128)}, u32[]{:S(2)}) copy-start(f32[2,32,2,8]{1,3,0,2:T(8,128)} %get-tuple-element.9) | copy-start | bytes 12292
  269.2 10.6 %copy-start.47 = (pred[2,32]{1,0:T(4,128)(4,1)S(1)}, pred[2,32]{1,0:T(4,128)(4,1)}, u32[]{:S(2)}) copy-start(pred[2,32]{1,0:T(4,128)(4,1)} %iota_compare_fusion.1) | copy-start | bytes 196
  276.8 15.2 %copy-start.36 = (f32[2048]{0:T(1024)S(1)}, f32[2048]{0:T(1024)}, u32[]{:S(2)}) copy-start(f32[2048]{0:T(1024)} %convert_element_type.46) | copy-start | bytes 24580
  (2 other events, 10.4 us)
Sparse Core Ops, SparseCore 0:
  10.1 80.7 all-gather.2
  93.7 118.4 all-gather.4
where the time goes:
time: 302 us; the launch traced here: 301 us
  waiting for transfers between devices  157 us (52%)
  local copies, waits for them, and re-layouts  53.9 us (18%)
  matrix products  38 us (13%)
  other arithmetic  26.4 us (9%)
  between operations  14.3 us (5%)
  blocking collectives  10.5 us (3%)
    all_gather x1, waiting for transfers between devices, on_device(): gathered = lax.all_gather(node_kv, 'branch', axis=0, tiled=True)  84.3 us
    all_gather x1, waiting for transfers between devices, on_device(): piece = lax.all_gather(root_kv, 'branch', axis=0, tiled=True)  72.4 us
    unnamed x100, local copies, waits for them, and re-layouts  21.3 us
    dot_general x10, matrix products, absorb(): jnp.einsum(form, weights.astype(jnp.bfloat16), values, preferred_element_...  20.6 us
    reduce_sum x9, other arithmetic, absorb(): total = total * factor + jnp.sum(weights, axis=-1)  17.3 us
    psum x1, blocking collectives, on_device(): squares = lax.psum(jnp.sum(attended * attended, axis=-1), 'blk')  10.5 us
    slice x1, local copies, waits for them, and re-layouts, on_device(): fold_values = piece[:, 1].reshape(piece.shape[0], kv_local, HEAD_DIM)  9.95 us
    slice x12, local copies, waits for them, and re-layouts, on_device(): values = level_blocks[:, :, 1].reshape(branches, block, kv_local, HEAD_DIM)  9.47 us
  transfers between devices with their start and end apart: 2, of which 2 were waited for; matrix products, arithmetic and copies ran while one was open for 16% of the time, Pallas kernels for 0%

commit v1 on v0

v1 whole, which is shorter than its diff:
```python
import functools
import math

import jax
import jax.numpy as jnp
from jax import lax
from jax.experimental import pallas as pl
from jax.experimental.pallas import tpu as pltpu
from jax.sharding import PartitionSpec as P

MESH = pl.DeviceIdType.MESH
HEADS = 64
DIM = 128
SEG = 32
GROUP = 8
SLOTS = 3
ROWS = GROUP * SEG
ROOT = 64
ZN = 8
XN = 4
C2 = math.log2(math.e) / math.sqrt(DIM)
NEG = -1e30
TAIL = 16
POS_DZ = (0, -1, 1, -2, 2, -3, 3, 4)
STAGES = ((0, 1, 2), (3, 4), (5, 6), (7,))
NPIECE = 6


def pos_of(step, direction):
    return 7 if step == 4 else 2 * step - 1 + direction


def kernel(
    q_hbm, root_x, node_x, own_x, owner_s, slot_s, depth_s, seg_s, gain_ref, out_ref,
    qbuf, rk, rv, rvt, ownk, ownv,
    n000, n001, n002, n003, n010, n011, n012, n013,
    n100, n101, n102, n103, n110, n111, n112, n113,
    acc, md, s0, s1, r0, r1, tbuf, tsm, sendbuf, recvbuf, att, ssq, ssq_in,
    zsend, zrecv, csend, crecv, qsend, qrecv, tsend, trecv, osend, orecv, ysend, yrecv, lsem,
):
    bf16, f32 = jnp.bfloat16, jnp.float32
    nodes = (
        ((n000, n001, n002, n003), (n010, n011, n012, n013)),
        ((n100, n101, n102, n103), (n110, n111, n112, n113)),
    )
    y = lax.axis_index("blk")
    r = lax.axis_index("branch")
    z, x, c = r // 8, (r // 2) % 4, r % 2

    def dev(dy=0, dz=0, dx=0, dc=0):
        zz = lax.rem(z + dz + ZN, ZN)
        xx = lax.rem(x + dx + XN, XN)
        cc = lax.rem(c + dc, 2)
        return (lax.rem(y + dy, 4), zz * 8 + xx * 2 + cc)

    bar = pltpu.get_barrier_semaphore()
    peers = [dev(dz=1), dev(dz=-1), dev(dc=1)]
    peers += [dev(dx=d) for d in (1, 2, 3)] + [dev(dy=d) for d in (1, 2, 3)]
    for p in peers:
        pl.semaphore_signal(bar, inc=1, device_id=p, device_id_type=MESH)

    qcopy = pltpu.make_async_copy(q_hbm, qbuf.at[3], lsem.at[0])
    qcopy.start()

    row = lax.broadcasted_iota(jnp.int32, (128, 128), 0)
    col = lax.broadcasted_iota(jnp.int32, (128, 128), 1)
    want = (row % 32) * 4 + row // 32
    pick = jnp.where(col == want, 1.0, 0.0).astype(bf16)

    def apart(ref, first):
        return jnp.dot(pick, ref[first : first + 128, :], preferred_element_type=f32)

    for t in range(2):
        got = apart(root_x, t * 128).astype(bf16)
        for h in range(2):
            rk[0, 0, h, t * 32 : t * 32 + 32, :] = got[h * 64 : h * 64 + 32]
            rv[0, 0, h, t * 32 : t * 32 + 32, :] = got[h * 64 + 32 : h * 64 + 64]
    for s in range(SLOTS):
        got = [apart(node_x, (s * 4 + t) * 128) for t in range(4)]
        for h in range(2):
            keys = jnp.concatenate([g[h * 64 : h * 64 + 32] for g in got], axis=0)
            vals = jnp.concatenate([g[h * 64 + 32 : h * 64 + 64] for g in got], axis=0)
            nodes[h][0][0][0, 0, s] = keys.astype(bf16)
            nodes[h][1][0][0, 0, s] = jnp.transpose(vals).astype(bf16)
    zeros96 = jnp.zeros((96, 128), f32)
    for b in range(2):
        got = apart(own_x, b * 128)
        for h in range(2):
            keys = jnp.concatenate([got[h * 64 : h * 64 + 32], zeros96], axis=0)
            vals = jnp.concatenate([got[h * 64 + 32 : h * 64 + 64], zeros96], axis=0)
            ownk[b, h] = keys.astype(bf16)
            ownv[b, h] = jnp.transpose(vals).astype(bf16)
    lane = lax.broadcasted_iota(jnp.int32, (8, 128), 1)
    sub = lax.broadcasted_iota(jnp.int32, (8, 128), 0)
    table = jnp.zeros((8, 128), jnp.int32)
    for b in range(2):
        for l in range(8):
            name = jnp.where(l < depth_s[b], owner_s[b, l], -1)
            table = jnp.where((lane == name) & (sub == b), slot_s[b, l] + 1, table)
    tbuf[3] = table

    pl.semaphore_wait(bar, len(peers))

    def view(piece, pos, core):
        if piece < 2:
            return (rk, rv)[piece].at[pos, core]
        for st, members in enumerate(STAGES):
            if pos in members:
                return nodes[piece // 2 - 1][piece % 2][st].at[members.index(pos), core]

    started = []

    def zcopy(piece, direction, step):
        src = view(piece, 0 if step == 1 else pos_of(step - 1, direction), 0)
        dst = view(piece, pos_of(step, direction), 0)
        return pltpu.make_async_remote_copy(
            src, dst, zsend.at[piece, direction, step - 1], zrecv.at[piece, direction, step - 1],
            device_id=dev(dz=1 if direction == 0 else -1), device_id_type=MESH,
        )

    def ccopy(piece, pos):
        return pltpu.make_async_remote_copy(
            view(piece, pos, 0), view(piece, pos, 1), csend.at[piece, pos], crecv.at[piece, pos],
            device_id=dev(dc=1), device_id_type=MESH,
        )

    def go(copy):
        copy.start()
        started.append(copy)

    def exists(piece, direction, step):
        return step <= 3 or (step == 4 and piece % 2 == direction)

    def begin(piece):
        for direction in (0, 1):
            go(zcopy(piece, direction, 1))
        go(ccopy(piece, 0))

    def forward(piece, step):
        for direction in (0, 1):
            if exists(piece, direction, step):
                zcopy(piece, direction, step).wait_recv()
                if exists(piece, direction, step + 1):
                    go(zcopy(piece, direction, step + 1))
                go(ccopy(piece, pos_of(step, direction)))

    def settle(piece, stage):
        for pos in STAGES[stage]:
            ccopy(piece, pos).wait_recv()

    def xcopies(j):
        to = dev(dx=j + 1)
        qc = pltpu.make_async_remote_copy(
            qbuf.at[3], qbuf.at[2 - j], qsend.at[j], qrecv.at[2 - j], device_id=to, device_id_type=MESH
        )
        tc = pltpu.make_async_remote_copy(
            tbuf.at[3], tbuf.at[2 - j], tsend.at[j], trecv.at[2 - j], device_id=to, device_id_type=MESH
        )
        return qc, tc

    begin(0)
    begin(1)
    for j in range(3):
        go(xcopies(j)[1])
    qcopy.wait()
    for j in (0, 2, 1):
        go(xcopies(j)[0])
    begin(2)
    begin(3)

    def queries_of(u, h):
        j, b = u // 2, u % 2
        parts = [qbuf[j, b, :, h * 1024 + g * 128 : h * 1024 + g * 128 + 128] for g in range(GROUP)]
        return jnp.concatenate(parts, axis=0)

    def scores_of(keys, q):
        return lax.dot_general(keys, q, (((1,), (1,)), ((), ())), preferred_element_type=f32)

    def with_ones(vt):
        return jnp.concatenate([vt, jnp.ones((TAIL, vt.shape[1]), bf16)], axis=0)

    def clear(u, _):
        for h in range(2):
            acc[u, h] = jnp.zeros((DIM + TAIL, ROWS), f32)
            md[u, h] = jnp.full((8, ROWS), NEG, f32)
        return 0

    lax.fori_loop(0, 6, clear, 0)
    key_at = lax.broadcasted_iota(jnp.int32, (128, ROWS), 0)
    query_at = lax.rem(lax.broadcasted_iota(jnp.int32, (128, ROWS), 1), SEG)
    causal = key_at <= query_at
    for b in range(2):
        for h in range(2):
            s = scores_of(ownk[b, h], queries_of(6 + b, h))
            s = jnp.where(causal, s, NEG)
            m = jnp.max(s, axis=0, keepdims=True)
            p = jnp.exp2(s * C2 - m * C2).astype(bf16)
            acc[6 + b, h] = jnp.dot(with_ones(ownv[b, h]), p, preferred_element_type=f32)
            md[6 + b, h] = jnp.broadcast_to(m, (8, ROWS))

    forward(0, 1)
    forward(1, 1)
    forward(0, 2)
    forward(1, 2)
    forward(0, 3)
    forward(1, 3)
    forward(2, 1)
    forward(3, 1)
    forward(0, 4)
    forward(1, 4)
    begin(4)
    begin(5)
    for j in range(3):
        xcopies(2 - j)[1].wait_recv()
    tcopy = pltpu.make_async_copy(tbuf, tsm, lsem.at[1])
    tcopy.start()
    for j in (2, 0, 1):
        xcopies(2 - j)[0].wait_recv()
    tcopy.wait()
    for st in range(4):
        settle(0, st)
        settle(1, st)
    for h in range(2):
        for p in range(ZN):
            pair = jnp.concatenate([rv[p, 0, h], rv[p, 1, h]], axis=0).astype(f32)
            rvt[h, :, p * 128 : p * 128 + 128] = jnp.transpose(pair).astype(bf16)

    sbuf, rbuf = (s0, s1), (r0, r1)

    def unit_a(u, h, t, keys, biases):
        q = queries_of(u, h)
        old = md[u, h, 0:1, :]
        top = old
        at = 0
        for k, bias in zip(keys, biases):
            s = scores_of(k, q)
            sbuf[t][at : at + k.shape[0], :] = s
            best = jnp.max(s, axis=0, keepdims=True)
            top = jnp.maximum(top, best if bias is None else best + bias)
            at += k.shape[0]
        md[u, h, 0:1, :] = top
        rbuf[t][0:1, :] = top * C2
        rbuf[t][1:2, :] = jnp.exp2((old - top) * C2)

    def unit_b(u, h, t, vts, biases):
        low, factor = rbuf[t][0:1, :], rbuf[t][1:2, :]
        weights = []
        at = 0
        for vt, bias in zip(vts, biases):
            width = vt.shape[1]
            less = low if bias is None else low - bias
            weights.append(jnp.exp2(sbuf[t][at : at + width, :] * C2 - less).astype(bf16))
            at += width
        p = weights[0] if len(weights) == 1 else jnp.concatenate(weights, axis=0)
        vt = vts[0] if len(vts) == 1 else jnp.concatenate(vts, axis=1)
        acc[u, h] = acc[u, h] * factor + jnp.dot(with_ones(vt), p, preferred_element_type=f32)

    def pipeline(unit_1, unit_2, after=None):
        unit_1(0, 0)

        def body(j, _):
            unit_1(2 * j + 1, 1)
            unit_2(2 * j, 0)
            if after is not None:
                after(2 * j)
            unit_1(2 * j + 2, 0)
            unit_2(2 * j + 1, 1)
            if after is not None:
                after(2 * j + 1)
            return 0

        lax.fori_loop(0, 3, body, 0)
        unit_1(7, 1)
        unit_2(6, 0)
        unit_2(7, 1)

    def root_stage(h):
        def first(u, t):
            unit_a(u, h, t, [jnp.concatenate([rk[p, core, h] for p in range(ZN) for core in range(2)], axis=0)], [None])

        def second(u, t):
            unit_b(u, h, t, [rvt[h]], [None])

        pipeline(first, second)

    def node_stage(h, st, after=None):
        members = [(i, pos, core) for i, pos in enumerate(STAGES[st]) for core in range(2)]

        def names(u):
            got = []
            for i, pos, core in members:
                zz = lax.rem(z + POS_DZ[pos] + ZN, ZN)
                owner = zz * 8 + x * 2 + (c if core == 0 else 1 - c)
                got.append(tsm[u // 2, u % 2, owner])
            biases = [jnp.where(g > 0, 0.0, NEG).astype(f32) for g in got]
            return [jnp.clip(g - 1, 0, SLOTS - 1) for g in got], biases

        def first(u, t):
            at, biases = names(u)
            unit_a(u, h, t, [nodes[h][0][st][i, core, a] for (i, _, core), a in zip(members, at)], biases)

        def second(u, t):
            at, biases = names(u)
            unit_b(u, h, t, [nodes[h][1][st][i, core, a] for (i, _, core), a in zip(members, at)], biases)

        pipeline(first, second, after)

    def three(v):
        a = v.astype(bf16).astype(f32)
        b = (v - a).astype(bf16).astype(f32)
        return [a, b, v - a - b]

    def ocopy(u, h):
        j, b = u // 2, u % 2
        return pltpu.make_async_remote_copy(
            sendbuf.at[h, j, b], recvbuf.at[h, 2 - j, b], osend.at[h, j, b], orecv.at[h, 2 - j, b],
            device_id=dev(dx=j + 1), device_id_type=MESH,
        )

    def send_part(h):
        def after(u):
            j, b = u // 2, u % 2
            sendbuf[h, j, b, :DIM, :] = acc[u, h, :DIM, :].astype(bf16)
            tail = three(md[u, h, 0:1, :]) + three(acc[u, h, DIM : DIM + 1, :])
            tail = jnp.concatenate(tail + [jnp.zeros((TAIL - 6, ROWS), f32)], axis=0)
            sendbuf[h, j, b, DIM:, :] = tail.astype(bf16)
            ocopy(u, h).start()

        return after

    def merge(h):
        for j in range(3):
            for b in range(2):
                ocopy(2 * (2 - j) + b, h).wait_recv()
        for b in range(2):
            tops, dens, sums = [md[6 + b, h, 0:1, :]], [acc[6 + b, h, DIM : DIM + 1, :]], [acc[6 + b, h, :DIM, :]]
            for j in range(3):
                tail = recvbuf[h, j, b, DIM:, :].astype(f32)
                tops.append(tail[0:1] + tail[1:2] + tail[2:3])
                dens.append(tail[3:4] + tail[4:5] + tail[5:6])
                sums.append(recvbuf[h, j, b, :DIM, :].astype(f32))
            top = functools.reduce(jnp.maximum, tops)
            ws = [jnp.exp2((t - top) * C2) for t in tops]
            den = sum(w * d for w, d in zip(ws, dens))
            inv = 1.0 / den
            total = sum(s * (w * inv) for s, w in zip(sums, ws))
            rows = jnp.transpose(total)
            live = lax.broadcasted_iota(jnp.int32, (SEG, DIM), 0) < seg_s[b]
            part = jnp.zeros((SEG, DIM), f32)
            for g in range(GROUP):
                one = jnp.where(live, rows[g * SEG : g * SEG + SEG, :], 0.0)
                att[b, :, h * 1024 + g * 128 : h * 1024 + g * 128 + 128] = one
                part = part + one * one
            part = jnp.broadcast_to(jnp.sum(part, axis=1, keepdims=True), (SEG, DIM))
            ssq[b] = part if h == 0 else ssq[b] + part

    root_stage(0)
    forward(2, 2)
    forward(3, 2)
    root_stage(1)
    forward(2, 3)
    forward(3, 3)
    settle(2, 0)
    settle(3, 0)
    node_stage(0, 0)
    forward(4, 1)
    forward(5, 1)
    forward(2, 4)
    forward(3, 4)
    settle(2, 1)
    settle(3, 1)
    node_stage(0, 1)
    forward(4, 2)
    forward(5, 2)
    settle(2, 2)
    settle(3, 2)
    node_stage(0, 2)
    settle(2, 3)
    settle(3, 3)
    node_stage(0, 3, send_part(0))
    forward(4, 3)
    forward(5, 3)
    settle(4, 0)
    settle(5, 0)
    node_stage(1, 0)
    forward(4, 4)
    forward(5, 4)
    settle(4, 1)
    settle(5, 1)
    node_stage(1, 1)
    settle(4, 2)
    settle(5, 2)
    node_stage(1, 2)
    merge(0)
    settle(4, 3)
    settle(5, 3)
    node_stage(1, 3, send_part(1))
    merge(1)

    def ycopy(d):
        return pltpu.make_async_remote_copy(
            ssq, ssq_in.at[3 - d], ysend.at[d - 1], yrecv.at[3 - d], device_id=dev(dy=d), device_id_type=MESH
        )

    for d in (1, 2, 3):
        go(ycopy(d))
    for d in (1, 2, 3):
        ycopy(d).wait_recv()
    for b in range(2):
        squares = ssq[b] + ssq_in[0, b] + ssq_in[1, b] + ssq_in[2, b]
        scale = lax.rsqrt(squares / (HEADS * DIM) + 1e-6)
        for g in range(2 * GROUP):
            at = slice(g * 128, g * 128 + 128)
            out_ref[b, :, at] = (att[b, :, at] * scale * gain_ref[:, at].astype(f32)).astype(bf16)

    for copy in started:
        copy.wait_send()
    for h in range(2):
        for u in range(6):
            ocopy(u, h).wait_send()


def on_device(queries, root_kv, node_kv, own_kv, anc_owner, anc_slot, depth_len, seg_len, norm_gain):
    bf16, f32 = jnp.bfloat16, jnp.float32

    def rows_of(kv):
        lead = kv.shape[:-2]
        n = len(lead)
        kv = kv.reshape(lead + (2, 2, DIM))
        kv = kv.transpose(tuple(range(n)) + (n + 1, n, n + 2))
        return kv.reshape(-1, DIM)

    vmem = pl.BlockSpec(memory_space=pltpu.VMEM)
    smem = pl.BlockSpec(memory_space=pltpu.SMEM)
    node_refs = [
        pltpu.VMEM((len(members), 2, SLOTS, 128, 128), bf16) for _ in range(4) for members in STAGES
    ]
    dma = pltpu.SemaphoreType.DMA
    scratch = [
        pltpu.VMEM((XN, 2, SEG, 2048), bf16),
        pltpu.VMEM((ZN, 2, 2, ROOT, DIM), bf16),
        pltpu.VMEM((ZN, 2, 2, ROOT, DIM), bf16),
        pltpu.VMEM((2, DIM, ZN * 2 * ROOT), bf16),
        pltpu.VMEM((2, 2, 128, DIM), bf16),
        pltpu.VMEM((2, 2, DIM, 128), bf16),
        *node_refs,
        pltpu.VMEM((8, 2, DIM + TAIL, ROWS), f32),
        pltpu.VMEM((8, 2, 8, ROWS), f32),
        pltpu.VMEM((1024, ROWS), f32),
        pltpu.VMEM((1024, ROWS), f32),
        pltpu.VMEM((8, ROWS), f32),
        pltpu.VMEM((8, ROWS), f32),
        pltpu.VMEM((XN, 8, 128), jnp.int32),
        pltpu.SMEM((XN, 8, 128), jnp.int32),
        pltpu.VMEM((2, 3, 2, DIM + TAIL, ROWS), bf16),
        pltpu.VMEM((2, 3, 2, DIM + TAIL, ROWS), bf16),
        pltpu.VMEM((2, SEG, 2048), f32),
        pltpu.VMEM((2, SEG, DIM), f32),
        pltpu.VMEM((3, 2, SEG, DIM), f32),
        dma((NPIECE, 2, 4)),
        dma((NPIECE, 2, 4)),
        dma((NPIECE, 8)),
        dma((NPIECE, 8)),
        dma((3,)),
        dma((3,)),
        dma((3,)),
        dma((3,)),
        dma((2, 3, 2)),
        dma((2, 3, 2)),
        dma((3,)),
        dma((3,)),
        dma((2,)),
    ]
    return pl.pallas_call(
        kernel,
        out_shape=jax.ShapeDtypeStruct(queries.shape, bf16),
        in_specs=[pl.BlockSpec(memory_space=pl.ANY), vmem, vmem, vmem, smem, smem, smem, smem, vmem],
        out_specs=vmem,
        scratch_shapes=scratch,
        compiler_params=pltpu.CompilerParams(
            collective_id=0, has_side_effects=True, vmem_limit_bytes=48 * 2**20
        ),
        name="tree_attention",
    )(
        queries, rows_of(root_kv), rows_of(node_kv), rows_of(own_kv),
        anc_owner, anc_slot, depth_len, seg_len, norm_gain.reshape(1, -1),
    )


def solution(mesh):
    in_specs = (
        P("branch", None, "blk"),
        P("branch", None, "blk"),
        P("branch", None, None, "blk"),
        P("branch", None, None, "blk"),
        P("branch", None),
        P("branch", None),
        P("branch"),
        P("branch"),
        P("blk"),
    )
    return jax.shard_map(
        on_device, mesh=mesh, in_specs=in_specs, out_specs=P("branch", None, "blk"), check_vma=False
    )
```

time: 302 us -> 79.8 us (0.26)
  waiting for transfers between devices: 157 us -> 0 us
  Pallas kernels: 0 us -> 73.8 us
  local copies, waits for them, and re-layouts: 53.9 us -> 5.7 us
  matrix products: 38 us -> 0 us
  other arithmetic: 26.4 us -> 0 us
  between operations: 14.3 us -> 0.03 us
  blocking collectives: 10.5 us -> 0 us
    all_gather x2 -> x0, waiting for transfers between devices: 157 us -> none  [the longest x1 84.3 us: on_device(): gathered = lax.all_gather(node_kv, 'branch', axis=0, tiled=True)]
    pallas_call x0 -> x1, Pallas kernels: none -> 73.8 us  [on_device(): pl.pallas_call(kernel, out_shape=jax.ShapeDtypeStruct(queries.shape, bf16...]
    dot_general x20 -> x0, matrix products: 38 us -> none  [the longest x10 20.6 us: absorb(): jnp.einsum(form, weights.astype(jnp.bfloat16), values, preferred_element_...]
    slice x22 -> x0, local copies, waits for them, and re-layouts: 21.6 us -> none  [the longest x1 9.95 us: on_device(): fold_values = piece[:, 1].reshape(piece.shape[0], kv_local, HEAD_DIM)]
    reduce_sum x9 -> x0, other arithmetic: 17.3 us -> none  [absorb(): total = total * factor + jnp.sum(weights, axis=-1)]
    unnamed x100 -> x19, local copies, waits for them, and re-layouts: 21.3 us -> 5.7 us
    psum x1 -> x0, blocking collectives: 10.5 us -> none  [on_device(): squares = lax.psum(jnp.sum(attended * attended, axis=-1), 'blk')]
    gather x1 -> x0, local copies, waits for them, and re-layouts: 8.84 us -> none  [on_device(): ancestors = gathered[node_ids].reshape(branches, depth, block, 2, kwidth)]
  transfers between devices with their start and end apart: 2 -> 0, of which waited for: 2 -> 0; matrix products, arithmetic and copies ran while one was open for 16% -> 0% of each run, Pallas kernels for 0% -> 0%
where the time goes in v1:
time: 79.8 us; the launch traced here: 79.5 us
  Pallas kernels  73.8 us (92%)
  local copies, waits for them, and re-layouts  5.7 us (7%)
    pallas_call x1, Pallas kernels, on_device(): pl.pallas_call(kernel, out_shape=jax.ShapeDtypeStruct(queries.shape, bf16...  73.8 us
    unnamed x19, local copies, waits for them, and re-layouts  5.7 us

profile of v1, /device:TPU:2, one launch (start us, length us, event | category | flops | bytes accessed | tf_op | source)
XLA Modules:
  0.0 79.5 jit_solution(18034588192389947708)
XLA Ops:
  0.0 0.0 copy-start.8
  0.0 0.7 copy-done.8
  0.7 0.0 copy-start.4
  0.7 0.0 copy-start.5
  0.7 0.0 copy-start.6
  0.7 0.0 copy-start.7
  0.7 0.7 copy-done.4
  1.4 0.0 copy-done.5
  1.4 0.0 copy-done.6
  1.4 0.0 copy-done.7
  1.4 0.0 copy-start
  1.4 1.0 %copy-done = bf16[3,128,2,256]{3,2,1,0:T(2,128)(2,1)S(1)} copy-done((bf16[3,128,2,256]{3,2,1,0:T(2,128)(2,1)S(1)}, bf16[3,128,2,256]{3,2,1,0:T(2,128)(2,1)}, u32[]{:S(2)}) %copy-start) | copy-done | bytes 393240
  2.4 0.0 copy-start.1
  2.4 0.9 %copy-done.1 = bf16[2,32,2048]{2,1,0:T(8,128)(2,1)S(1)} copy-done((bf16[2,32,2048]{2,1,0:T(8,128)(2,1)S(1)}, bf16[2,32,2048]{2,1,0:T(8,128)(2,1)}, u32[]{:S(2)}) %copy-start.1) | copy-done | bytes 262168
  3.3 0.0 copy-start.2
  3.3 0.8 %copy-done.2 = bf16[64,2,256]{2,1,0:T(2,128)(2,1)S(1)} copy-done((bf16[64,2,256]{2,1,0:T(2,128)(2,1)S(1)}, bf16[64,2,256]{2,1,0:T(2,128)(2,1)}, u32[]{:S(2)}) %copy-start.2) | copy-done | bytes 65560
  4.2 0.0 copy-start.3
  4.2 0.8 %copy-done.3 = bf16[2,32,2,256]{3,2,1,0:T(2,128)(2,1)S(1)} copy-done((bf16[2,32,2,256]{3,2,1,0:T(2,128)(2,1)S(1)}, bf16[2,32,2,256]{3,2,1,0:T(2,128)(2,1)}, u32[]{:S(2)}) %copy-start.3) | copy-done | bytes 65560
  5.0 73.8 %tree_attention.1 = bf16[2,32,2048]{2,1,0:T(8,128)(2,1)S(1)} custom-call(bf16[2,32,2048]{2,1,0:T(8,128)(2,1)S(1)} %copy-done.1, bf16[256,128]{1,0:T(8,128)(2,1)S(1)} %bitcast.16, bf16[1536,128]{1,0:T(8,128)(2,1)S(1)} %bitcast.15, bf16[256,128]{1,0:T(8,128)(2,1)S(1)} %bitcast.17, s32[2,8]{1,0:T(2,128)S(1)} %copy-done.4, s32[2,8]{1,0:T(2,128)S(1)} %copy-done.5, ...), custom_call_target="tpu_custom_call" | custom-call | tf_op jit(solution)/shard_map/tree_attention/pallas_call | solution.py:474
  78.8 0.7 copy.14
  (1 shorter events, 0.0 us)
Async XLA Ops:
  0.0 0.7 copy-start.8
  0.7 0.7 copy-start.4
  0.7 0.7 copy-start.5
  0.7 0.7 copy-start.6
  0.7 0.7 copy-start.7
  1.4 1.0 %copy-start = (bf16[3,128,2,256]{3,2,1,0:T(2,128)(2,1)S(1)}, bf16[3,128,2,256]{3,2,1,0:T(2,128)(2,1)}, u32[]{:S(2)}) copy-start(bf16[3,128,2,256]{3,2,1,0:T(2,128)(2,1)} %param.11) | copy-start | bytes 1179652
  2.4 0.9 %copy-start.1 = (bf16[2,32,2048]{2,1,0:T(8,128)(2,1)S(1)}, bf16[2,32,2048]{2,1,0:T(8,128)(2,1)}, u32[]{:S(2)}) copy-start(bf16[2,32,2048]{2,1,0:T(8,128)(2,1)} %q_hbm.1) | copy-start | bytes 786436
  3.3 0.8 %copy-start.2 = (bf16[64,2,256]{2,1,0:T(2,128)(2,1)S(1)}, bf16[64,2,256]{2,1,0:T(2,128)(2,1)}, u32[]{:S(2)}) copy-start(bf16[64,2,256]{2,1,0:T(2,128)(2,1)} %param.10) | copy-start | bytes 196612
  4.2 0.8 %copy-start.3 = (bf16[2,32,2,256]{3,2,1,0:T(2,128)(2,1)S(1)}, bf16[2,32,2,256]{3,2,1,0:T(2,128)(2,1)}, u32[]{:S(2)}) copy-start(bf16[2,32,2,256]{3,2,1,0:T(2,128)(2,1)} %param.12) | copy-start | bytes 196612

commit v2 on v1

v2 whole, which is shorter than its diff:
```python
import functools
import math

import jax
import jax.numpy as jnp
from jax import lax
from jax.experimental import pallas as pl
from jax.experimental.pallas import tpu as pltpu
from jax.sharding import PartitionSpec as P

MESH = pl.DeviceIdType.MESH
HEADS = 64
DIM = 128
SEG = 32
GROUP = 8
SLOTS = 3
ROWS = GROUP * SEG
ROOT = 64
ZN = 8
XN = 4
C2 = math.log2(math.e) / math.sqrt(DIM)
NEG = -1e30
TAIL = 16
POS_DZ = (0, -1, 1, -2, 2, -3, 3, 4)
STAGES = ((3, 1, 0, 2, 4), (5, 6), (7,))
NEAR = len(STAGES[0])
NPIECE = 6


def pos_of(step, direction):
    return 7 if step == 4 else 2 * step - 1 + direction


def kernel(
    q_hbm, root_hbm, node_hbm, own_hbm, owner_hbm, slot_hbm, depth_hbm, seg_hbm, gain_hbm, out_ref,
    root_x, node_x, own_x, owner_s, slot_s, depth_s, seg_s, gain_ref,
    qbuf, rk, rv, rvt, ownk, ownv,
    n000, n001, n002, n010, n011, n012, n100, n101, n102, n110, n111, n112,
    acc, md, s0, s1, r0, r1, tbuf, tsm, sendbuf, recvbuf, att, ssq, ssq_in,
    zsend, zrecv, csend, crecv, qsend, qrecv, tsend, trecv, osend, orecv, ysend, yrecv, lsem,
):
    bf16, f32 = jnp.bfloat16, jnp.float32
    nodes = (
        ((n000, n001, n002), (n010, n011, n012)),
        ((n100, n101, n102), (n110, n111, n112)),
    )
    y = lax.axis_index("blk")
    r = lax.axis_index("branch")
    z, x, c = r // 8, (r // 2) % 4, r % 2

    def dev(dy=0, dz=0, dx=0, dc=0):
        zz = lax.rem(z + dz + ZN, ZN)
        xx = lax.rem(x + dx + XN, XN)
        cc = lax.rem(c + dc, 2)
        return (lax.rem(y + dy, 4), zz * 8 + xx * 2 + cc)

    bar = pltpu.get_barrier_semaphore()
    peers = [dev(dz=1), dev(dz=-1), dev(dc=1)]
    peers += [dev(dx=d) for d in (1, 2, 3)] + [dev(dy=d) for d in (1, 2, 3)]
    for p in peers:
        pl.semaphore_signal(bar, inc=1, device_id=p, device_id_type=MESH)

    up, down, other = dev(dz=1), dev(dz=-1), dev(dc=1)

    def local(i, src, dst):
        copy = pltpu.make_async_copy(src, dst, lsem.at[i])
        copy.start()
        return copy

    node_in = local(0, node_hbm, node_x)
    root_in = local(1, root_hbm, root_x)
    small_in = [
        local(2, owner_hbm, owner_s), local(3, slot_hbm, slot_s), local(4, depth_hbm, depth_s), local(5, seg_hbm, seg_s)
    ]
    q_in = local(6, q_hbm, qbuf.at[3])
    own_in = local(7, own_hbm, own_x)
    gain_in = local(8, gain_hbm, gain_ref)

    row = lax.broadcasted_iota(jnp.int32, (128, 128), 0)
    col = lax.broadcasted_iota(jnp.int32, (128, 128), 1)
    want = (row % 32) * 4 + row // 32
    pick = jnp.where(col == want, 1.0, 0.0).astype(bf16)

    def apart(ref, first):
        return jnp.dot(pick, ref[first : first + 128, :], preferred_element_type=f32)

    def prepare_root():
        for t in range(2):
            got = apart(root_x, t * 128).astype(bf16)
            for h in range(2):
                rk[0, 0, h, t * 32 : t * 32 + 32, :] = got[h * 64 : h * 64 + 32]
                rv[0, 0, h, t * 32 : t * 32 + 32, :] = got[h * 64 + 32 : h * 64 + 64]

    def prepare_nodes():
        for s in range(SLOTS):
            got = [apart(node_x, (s * 4 + t) * 128) for t in range(4)]
            for h in range(2):
                keys = jnp.concatenate([g[h * 64 : h * 64 + 32] for g in got], axis=0)
                vals = jnp.concatenate([g[h * 64 + 32 : h * 64 + 64] for g in got], axis=0)
                nodes[h][0][0][2, 0, s] = keys.astype(bf16)
                nodes[h][1][0][2, 0, s] = jnp.transpose(vals).astype(bf16)

    def prepare_own():
        zeros96 = jnp.zeros((96, 128), f32)
        for b in range(2):
            got = apart(own_x, b * 128)
            for h in range(2):
                keys = jnp.concatenate([got[h * 64 : h * 64 + 32], zeros96], axis=0)
                vals = jnp.concatenate([got[h * 64 + 32 : h * 64 + 64], zeros96], axis=0)
                ownk[b, h] = keys.astype(bf16)
                ownv[b, h] = jnp.transpose(vals).astype(bf16)

    def prepare_table():
        lane = lax.broadcasted_iota(jnp.int32, (8, 128), 1)
        sub = lax.broadcasted_iota(jnp.int32, (8, 128), 0)
        table = jnp.zeros((8, 128), jnp.int32)
        for b in range(2):
            for l in range(8):
                name = jnp.where(l < depth_s[b], owner_s[b, l], -1)
                code = jnp.where(l < depth_s[b], 4 * owner_s[b, l] + slot_s[b, l] + 1, 0)
                table = jnp.where((lane == name) & (sub == 2 + b), slot_s[b, l] + 1, table)
                table = jnp.where((lane == l) & (sub == b), code, table)
        tbuf[3] = table

    root_in.wait()
    prepare_root()
    node_in.wait()
    prepare_nodes()
    for copy in small_in:
        copy.wait()
    prepare_table()
    q_in.wait()

    pl.semaphore_wait(bar, len(peers))

    def view(piece, pos, core):
        if piece < 2:
            return (rk, rv)[piece].at[pos, core]
        for st, members in enumerate(STAGES):
            if pos in members:
                return nodes[piece // 2 - 1][piece % 2][st].at[members.index(pos), core]

    started = []

    def zcopy(piece, direction, step):
        src = view(piece, 0 if step == 1 else pos_of(step - 1, direction), 0)
        dst = view(piece, pos_of(step, direction), 0)
        return pltpu.make_async_remote_copy(
            src, dst, zsend.at[piece, direction, step - 1], zrecv.at[piece, direction, step - 1],
            device_id=up if direction == 0 else down, device_id_type=MESH,
        )

    def ccopy(piece, pos):
        return pltpu.make_async_remote_copy(
            view(piece, pos, 0), view(piece, pos, 1), csend.at[piece, pos], crecv.at[piece, pos],
            device_id=other, device_id_type=MESH,
        )

    def go(copy):
        copy.start()
        started.append(copy)

    def send_own(kind, which):
        for direction in (0, 1):
            go(zcopy(2 * kind + (which ^ direction), direction, 1))

    def hop(kind, which, step):
        for direction in (0, 1):
            piece = 2 * kind + (which ^ direction)
            zcopy(piece, direction, step).wait_recv()
            if step < 3 or (step == 3 and which == 0):
                go(zcopy(piece, direction, step + 1))
            go(ccopy(piece, pos_of(step, direction)))

    def settle(kind, positions):
        for pos in positions:
            for piece in (2 * kind, 2 * kind + 1):
                ccopy(piece, pos).wait_recv()

    def qcopy(j):
        return pltpu.make_async_remote_copy(
            qbuf.at[3], qbuf.at[2 - j], qsend.at[j], qrecv.at[2 - j], device_id=dev(dx=j + 1), device_id_type=MESH
        )

    def tcopy(j):
        return pltpu.make_async_remote_copy(
            tbuf.at[3], tbuf.at[2 - j], tsend.at[j], trecv.at[2 - j], device_id=dev(dx=j + 1), device_id_type=MESH
        )

    send_own(0, 0)
    send_own(0, 1)
    send_own(1, 0)
    for j in range(3):
        go(tcopy(j))
    for j in (0, 2, 1):
        go(qcopy(j))
    for piece in range(NPIECE):
        go(ccopy(piece, 0))
    own_in.wait()
    prepare_own()
    hop(0, 0, 1)
    hop(0, 1, 1)
    send_own(1, 1)

    def queries_of(u, h):
        j, b = u // 2, u % 2
        parts = [qbuf[j, b, :, h * 1024 + g * 128 : h * 1024 + g * 128 + 128] for g in range(GROUP)]
        return jnp.concatenate(parts, axis=0)

    def scores_of(keys, q):
        return lax.dot_general(keys, q, (((1,), (1,)), ((), ())), preferred_element_type=f32)

    def with_ones(vt):
        return jnp.concatenate([vt, jnp.ones((TAIL, vt.shape[1]), bf16)], axis=0)

    def clear(u, _):
        for h in range(2):
            acc[u, h] = jnp.zeros((DIM + TAIL, ROWS), f32)
            md[u, h] = jnp.full((8, ROWS), NEG, f32)
        return 0

    lax.fori_loop(0, 6, clear, 0)
    key_at = lax.broadcasted_iota(jnp.int32, (128, ROWS), 0)
    query_at = lax.rem(lax.broadcasted_iota(jnp.int32, (128, ROWS), 1), SEG)
    causal = key_at <= query_at
    for b in range(2):
        for h in range(2):
            s = scores_of(ownk[b, h], queries_of(6 + b, h))
            s = jnp.where(causal, s, NEG)
            m = jnp.max(s, axis=0, keepdims=True)
            p = jnp.exp2(s * C2 - m * C2).astype(bf16)
            acc[6 + b, h] = jnp.dot(with_ones(ownv[b, h]), p, preferred_element_type=f32)
            md[6 + b, h] = jnp.broadcast_to(m, (8, ROWS))

    hop(0, 0, 2)
    hop(0, 1, 2)
    send_own(2, 0)
    hop(0, 0, 3)
    hop(0, 1, 3)
    send_own(2, 1)
    hop(1, 0, 1)
    hop(1, 1, 1)
    hop(2, 0, 1)
    for j in range(3):
        tcopy(2 - j).wait_recv()
    t_in = local(9, tbuf, tsm)
    hop(0, 0, 4)
    for j in (2, 0, 1):
        qcopy(2 - j).wait_recv()
    t_in.wait()
    settle(0, range(ZN))
    for h in range(2):
        for p in range(ZN):
            pair = jnp.concatenate([rv[p, 0, h], rv[p, 1, h]], axis=0).astype(f32)
            rvt[h, :, p * 128 : p * 128 + 128] = jnp.transpose(pair).astype(bf16)

    sbuf, rbuf = (s0, s1), (r0, r1)

    def unit_a(u, h, t, keys, biases):
        q = queries_of(u, h)
        old = md[u, h, 0:1, :]
        top = old
        s = scores_of(keys[0] if len(keys) == 1 else jnp.concatenate(keys, axis=0), q)
        sbuf[t][0 : s.shape[0], :] = s
        at = 0
        for k, bias in zip(keys, biases):
            best = jnp.max(s[at : at + k.shape[0]], axis=0, keepdims=True)
            top = jnp.maximum(top, best if bias is None else best + bias)
            at += k.shape[0]
        md[u, h, 0:1, :] = top
        rbuf[t][0:1, :] = top * C2
        rbuf[t][1:2, :] = jnp.exp2((old - top) * C2)

    def unit_b(u, h, t, vts, biases):
        low, factor = rbuf[t][0:1, :], rbuf[t][1:2, :]
        weights = []
        at = 0
        for vt, bias in zip(vts, biases):
            width = vt.shape[1]
            less = low if bias is None else low - bias
            weights.append(jnp.exp2(sbuf[t][at : at + width, :] * C2 - less).astype(bf16))
            at += width
        p = weights[0] if len(weights) == 1 else jnp.concatenate(weights, axis=0)
        vt = vts[0] if len(vts) == 1 else jnp.concatenate(vts, axis=1)
        acc[u, h] = acc[u, h] * factor + jnp.dot(with_ones(vt), p, preferred_element_type=f32)

    def pipeline(unit_1, unit_2, after=None, hooks=()):
        unit_1(0, 0)

        def body(j, _):
            unit_1(2 * j + 1, 1)
            unit_2(2 * j, 0)
            if after is not None:
                after(2 * j)
            unit_1(2 * j + 2, 0)
            unit_2(2 * j + 1, 1)
            if after is not None:
                after(2 * j + 1)
            return 0

        at = 0
        for when, hook in hooks:
            lax.fori_loop(at, when, body, 0)
            hook()
            at = when
        lax.fori_loop(at, 3, body, 0)
        unit_1(7, 1)
        unit_2(6, 0)
        unit_2(7, 1)

    def root_stage(h, hooks=()):
        def first(u, t):
            unit_a(u, h, t, [jnp.concatenate([rk[p, core, h] for p in range(ZN) for core in range(2)], axis=0)], [None])

        def second(u, t):
            unit_b(u, h, t, [rvt[h]], [None])

        pipeline(first, second, None, hooks)

    def bias_of(active):
        return jnp.where(active, 0.0, NEG).astype(f32)

    def near_stage(h, hooks=()):
        def names(u):
            got, biases = [], []
            for l in range(8):
                code = tsm[u // 2, u % 2, l]
                owner = code >> 2
                at = ((owner >> 3) - z + (2 + ZN)) & (ZN - 1)
                core = (owner + c) & 1
                mine = (code > 0) & (((owner >> 1) & (XN - 1)) == x) & (at < NEAR)
                biases.append(bias_of(mine))
                got.append((jnp.clip(at, 0, NEAR - 1), core, jnp.clip((code & 3) - 1, 0, SLOTS - 1)))
            return got, biases

        def first(u, t):
            at, biases = names(u)
            unit_a(u, h, t, [nodes[h][0][0][a] for a in at], biases)

        def second(u, t):
            at, biases = names(u)
            unit_b(u, h, t, [nodes[h][1][0][a] for a in at], biases)

        pipeline(first, second, None, hooks)

    def far_stage(h, st, after=None, hooks=()):
        members = [(i, pos, core) for i, pos in enumerate(STAGES[st]) for core in range(2)]

        def names(u):
            got = []
            for i, pos, core in members:
                zz = lax.rem(z + POS_DZ[pos] + ZN, ZN)
                owner = zz * 8 + x * 2 + (c if core == 0 else 1 - c)
                got.append(tsm[u // 2, 2 + u % 2, owner])
            return [jnp.clip(g - 1, 0, SLOTS - 1) for g in got], [bias_of(g > 0) for g in got]

        def first(u, t):
            at, biases = names(u)
            unit_a(u, h, t, [nodes[h][0][st][i, core, a] for (i, _, core), a in zip(members, at)], biases)

        def second(u, t):
            at, biases = names(u)
            unit_b(u, h, t, [nodes[h][1][st][i, core, a] for (i, _, core), a in zip(members, at)], biases)

        pipeline(first, second, after, hooks)

    def three(v):
        a = v.astype(bf16).astype(f32)
        b = (v - a).astype(bf16).astype(f32)
        return [a, b, v - a - b]

    def ocopy(u, h):
        j, b = u // 2, u % 2
        return pltpu.make_async_remote_copy(
            sendbuf.at[h, j, b], recvbuf.at[h, 2 - j, b], osend.at[h, j, b], orecv.at[h, 2 - j, b],
            device_id=dev(dx=j + 1), device_id_type=MESH,
        )

    def send_part(h):
        def after(u):
            j, b = u // 2, u % 2
            sendbuf[h, j, b, :DIM, :] = acc[u, h, :DIM, :].astype(bf16)
            tail = three(md[u, h, 0:1, :]) + three(acc[u, h, DIM : DIM + 1, :])
            tail = jnp.concatenate(tail + [jnp.zeros((TAIL - 6, ROWS), f32)], axis=0)
            sendbuf[h, j, b, DIM:, :] = tail.astype(bf16)
            ocopy(u, h).start()

        return after

    def merge(h):
        for j in range(3):
            for b in range(2):
                ocopy(2 * (2 - j) + b, h).wait_recv()
        for b in range(2):
            tops, dens, sums = [md[6 + b, h, 0:1, :]], [acc[6 + b, h, DIM : DIM + 1, :]], [acc[6 + b, h, :DIM, :]]
            for j in range(3):
                tail = recvbuf[h, j, b, DIM:, :].astype(f32)
                tops.append(tail[0:1] + tail[1:2] + tail[2:3])
                dens.append(tail[3:4] + tail[4:5] + tail[5:6])
                sums.append(recvbuf[h, j, b, :DIM, :].astype(f32))
            top = functools.reduce(jnp.maximum, tops)
            ws = [jnp.exp2((t - top) * C2) for t in tops]
            den = sum(w * d for w, d in zip(ws, dens))
            inv = 1.0 / den
            total = sum(s * (w * inv) for s, w in zip(sums, ws))
            live = lax.rem(lax.broadcasted_iota(jnp.int32, (1, ROWS), 1), SEG) < seg_s[b]
            total = jnp.where(live, total, 0.0)
            part = jnp.sum(total * total, axis=0, keepdims=True)
            ssq[b : b + 1, :] = part if h == 0 else ssq[b : b + 1, :] + part
            rows = jnp.transpose(total)
            for g in range(GROUP):
                at = h * 1024 + g * 128
                att[b, :, at : at + 128] = rows[g * SEG : g * SEG + SEG, :]

    root_stage(0)
    hop(1, 0, 2)
    root_stage(1, [(1, lambda: hop(1, 1, 2))])
    settle(1, (0, 1, 2, 3, 4))

    def hook_a():
        hop(1, 0, 3)
        hop(2, 1, 1)

    near_stage(0, [(1, hook_a)])
    hop(1, 1, 3)
    settle(1, (5, 6))
    far_stage(0, 1, None, [(1, lambda: hop(2, 0, 2))])
    hop(1, 0, 4)
    settle(1, (7,))
    far_stage(0, 2, send_part(0))
    hop(2, 1, 2)
    settle(2, (0, 1, 2, 3, 4))
    near_stage(1, [(1, lambda: hop(2, 0, 3)), (2, lambda: hop(2, 1, 3))])
    settle(2, (5, 6))
    far_stage(1, 1, None, [(1, lambda: hop(2, 0, 4))])
    settle(2, (7,))
    far_stage(1, 2, send_part(1))
    merge(0)
    merge(1)

    def ycopy(d):
        return pltpu.make_async_remote_copy(
            ssq, ssq_in.at[3 - d], ysend.at[d - 1], yrecv.at[3 - d], device_id=dev(dy=d), device_id_type=MESH
        )

    for d in (1, 2, 3):
        go(ycopy(d))
    for d in (1, 2, 3):
        ycopy(d).wait_recv()
    gain_in.wait()
    squares = jnp.transpose(ssq[...] + ssq_in[0] + ssq_in[1] + ssq_in[2])
    squares = sum(squares[g * SEG : g * SEG + SEG, :] for g in range(GROUP))
    scales = lax.rsqrt(squares / (HEADS * DIM) + 1e-6)
    for b in range(2):
        scale = scales[:, b : b + 1]
        for g in range(2 * GROUP):
            at = slice(g * 128, g * 128 + 128)
            out_ref[b, :, at] = (att[b, :, at] * scale * gain_ref[at].astype(f32).reshape(1, DIM)).astype(bf16)

    for copy in started:
        copy.wait_send()
    for h in range(2):
        for u in range(6):
            ocopy(u, h).wait_send()


def on_device(queries, root_kv, node_kv, own_kv, anc_owner, anc_slot, depth_len, seg_len, norm_gain):
    bf16, f32 = jnp.bfloat16, jnp.float32

    def rows_of(kv):
        lead = kv.shape[:-2]
        n = len(lead)
        kv = kv.reshape(lead + (2, 2, DIM))
        kv = kv.transpose(tuple(range(n)) + (n + 1, n, n + 2))
        return kv.reshape(-1, DIM)

    node_refs = [
        pltpu.VMEM((len(members), 2, SLOTS, 128, 128), bf16) for _ in range(4) for members in STAGES
    ]
    dma = pltpu.SemaphoreType.DMA
    scratch = [
        pltpu.VMEM((2 * 2 * ROOT, DIM), bf16),
        pltpu.VMEM((SLOTS * 2 * 2 * 128, DIM), bf16),
        pltpu.VMEM((2 * 2 * 2 * SEG, DIM), bf16),
        pltpu.SMEM((2, 8), jnp.int32),
        pltpu.SMEM((2, 8), jnp.int32),
        pltpu.SMEM((2,), jnp.int32),
        pltpu.SMEM((2,), jnp.int32),
        pltpu.VMEM((2048,), bf16),
        pltpu.VMEM((XN, 2, SEG, 2048), bf16),
        pltpu.VMEM((ZN, 2, 2, ROOT, DIM), bf16),
        pltpu.VMEM((ZN, 2, 2, ROOT, DIM), bf16),
        pltpu.VMEM((2, DIM, ZN * 2 * ROOT), bf16),
        pltpu.VMEM((2, 2, 128, DIM), bf16),
        pltpu.VMEM((2, 2, DIM, 128), bf16),
        *node_refs,
        pltpu.VMEM((8, 2, DIM + TAIL, ROWS), f32),
        pltpu.VMEM((8, 2, 8, ROWS), f32),
        pltpu.VMEM((1024, ROWS), f32),
        pltpu.VMEM((1024, ROWS), f32),
        pltpu.VMEM((8, ROWS), f32),
        pltpu.VMEM((8, ROWS), f32),
        pltpu.VMEM((XN, 8, 128), jnp.int32),
        pltpu.SMEM((XN, 8, 128), jnp.int32),
        pltpu.VMEM((2, 3, 2, DIM + TAIL, ROWS), bf16),
        pltpu.VMEM((2, 3, 2, DIM + TAIL, ROWS), bf16),
        pltpu.VMEM((2, SEG, 2048), f32),
        pltpu.VMEM((8, ROWS), f32),
        pltpu.VMEM((3, 8, ROWS), f32),
        dma((NPIECE, 2, 4)),
        dma((NPIECE, 2, 4)),
        dma((NPIECE, 8)),
        dma((NPIECE, 8)),
        dma((3,)),
        dma((3,)),
        dma((3,)),
        dma((3,)),
        dma((2, 3, 2)),
        dma((2, 3, 2)),
        dma((3,)),
        dma((3,)),
        dma((10,)),
    ]
    return pl.pallas_call(
        kernel,
        out_shape=jax.ShapeDtypeStruct(queries.shape, bf16),
        in_specs=[pl.BlockSpec(memory_space=pltpu.HBM)] * 9,
        out_specs=pl.BlockSpec(memory_space=pltpu.VMEM),
        scratch_shapes=scratch,
        compiler_params=pltpu.CompilerParams(
            collective_id=0, has_side_effects=True, vmem_limit_bytes=64 * 2**20
        ),
        name="tree_attention",
    )(
        queries, rows_of(root_kv), rows_of(node_kv), rows_of(own_kv),
        anc_owner, anc_slot, depth_len, seg_len, norm_gain,
    )


def solution(mesh):
    in_specs = (
        P("branch", None, "blk"),
        P("branch", None, "blk"),
        P("branch", None, None, "blk"),
        P("branch", None, None, "blk"),
        P("branch", None),
        P("branch", None),
        P("branch"),
        P("branch"),
        P("blk"),
    )
    return jax.shard_map(
        on_device, mesh=mesh, in_specs=in_specs, out_specs=P("branch", None, "blk"), check_vma=False
    )
```

time: 79.8 us -> 68.7 us (0.86)
  Pallas kernels: 73.8 us -> 66.6 us
  local copies, waits for them, and re-layouts: 5.7 us -> 1.67 us
    pallas_call x1, Pallas kernels: 73.8 us -> 66.6 us  [on_device(): pl.pallas_call(kernel, out_shape=jax.ShapeDtypeStruct(queries.shape, bf16...]
    unnamed x19 -> x1, local copies, waits for them, and re-layouts: 5.7 us -> 1.67 us
where the time goes in v2:
time: 68.7 us; the launch traced here: 68.3 us
  Pallas kernels  66.6 us (97%)
  local copies, waits for them, and re-layouts  1.67 us (2%)
    pallas_call x1, Pallas kernels, on_device(): pl.pallas_call(kernel, out_shape=jax.ShapeDtypeStruct(queries.shape, bf16...  66.6 us
    unnamed x1, local copies, waits for them, and re-layouts  1.67 us

profile of v2, /device:TPU:2, one launch (start us, length us, event | category | flops | bytes accessed | tf_op | source)
XLA Modules:
  0.0 68.3 jit_solution(14628023166470941864)
XLA Ops:
  0.0 66.6 %tree_attention.1 = bf16[2,32,2048]{2,1,0:T(8,128)(2,1)} custom-call(bf16[2,32,2048]{2,1,0:T(8,128)(2,1)} %q_hbm.1, bf16[256,128]{1,0:T(8,128)(2,1)} %bitcast.16, bf16[1536,128]{1,0:T(8,128)(2,1)} %bitcast.15, bf16[256,128]{1,0:T(8,128)(2,1)} %bitcast.17, s32[2,8]{1,0:T(2,128)} %owner_hbm.1, s32[2,8]{1,0:T(2,128)} %slot_hbm.1, s32[2]{0:T(128)} %depth_hbm.1, ...), custom_call_target="tpu_custom_call" | custom-call | tf_op jit(solution)/shard_map/tree_attention/pallas_call | solution.py:524
  66.6 1.7 %copy.14 = bf16[2,32,2048]{2,1,0:T(8,128)(2,1)} copy(bf16[2,32,2048]{2,1,0:T(8,128)(2,1)} %tree_attention.1) | data formatting | bytes 524288

commit v3 on v2

--- a/solution.py
+++ b/solution.py
@@ -22,8 +22,7 @@
 NEG = -1e30
 TAIL = 16
 POS_DZ = (0, -1, 1, -2, 2, -3, 3, 4)
-STAGES = ((3, 1, 0, 2, 4), (5, 6), (7,))
-NEAR = len(STAGES[0])
+SLOT_DX = (2, 1, 3)
 NPIECE = 6
 
 
@@ -35,15 +34,12 @@
     q_hbm, root_hbm, node_hbm, own_hbm, owner_hbm, slot_hbm, depth_hbm, seg_hbm, gain_hbm, out_ref,
     root_x, node_x, own_x, owner_s, slot_s, depth_s, seg_s, gain_ref,
     qbuf, rk, rv, rvt, ownk, ownv,
-    n000, n001, n002, n010, n011, n012, n100, n101, n102, n110, n111, n112,
+    n00, n01, n10, n11,
     acc, md, s0, s1, r0, r1, tbuf, tsm, sendbuf, recvbuf, att, ssq, ssq_in,
     zsend, zrecv, csend, crecv, qsend, qrecv, tsend, trecv, osend, orecv, ysend, yrecv, lsem,
 ):
     bf16, f32 = jnp.bfloat16, jnp.float32
-    nodes = (
-        ((n000, n001, n002), (n010, n011, n012)),
-        ((n100, n101, n102), (n110, n111, n112)),
-    )
+    nodes = ((n00, n01), (n10, n11))
     y = lax.axis_index("blk")
     r = lax.axis_index("branch")
     z, x, c = r // 8, (r // 2) % 4, r % 2
@@ -72,7 +68,7 @@
     small_in = [
         local(2, owner_hbm, owner_s), local(3, slot_hbm, slot_s), local(4, depth_hbm, depth_s), local(5, seg_hbm, seg_s)
     ]
-    q_in = local(6, q_hbm, qbuf.at[3])
+    q_in = local(6, q_hbm, qbuf.at[pl.ds(6, 2)])
     own_in = local(7, own_hbm, own_x)
     gain_in = local(8, gain_hbm, gain_ref)
 
@@ -91,14 +87,15 @@
                 rk[0, 0, h, t * 32 : t * 32 + 32, :] = got[h * 64 : h * 64 + 32]
                 rv[0, 0, h, t * 32 : t * 32 + 32, :] = got[h * 64 + 32 : h * 64 + 64]
 
-    def prepare_nodes():
+    def prepare_nodes(keys_of, values_of):
         for s in range(SLOTS):
             got = [apart(node_x, (s * 4 + t) * 128) for t in range(4)]
-            for h in range(2):
+            for h in keys_of:
                 keys = jnp.concatenate([g[h * 64 : h * 64 + 32] for g in got], axis=0)
+                nodes[h][0][0, 0, s] = keys.astype(bf16)
+            for h in values_of:
                 vals = jnp.concatenate([g[h * 64 + 32 : h * 64 + 64] for g in got], axis=0)
-                nodes[h][0][0][2, 0, s] = keys.astype(bf16)
-                nodes[h][1][0][2, 0, s] = jnp.transpose(vals).astype(bf16)
+                nodes[h][1][0, 0, s] = jnp.transpose(vals).astype(bf16)
 
     def prepare_own():
         zeros96 = jnp.zeros((96, 128), f32)
@@ -116,29 +113,21 @@
         table = jnp.zeros((8, 128), jnp.int32)
         for b in range(2):
             for l in range(8):
-                name = jnp.where(l < depth_s[b], owner_s[b, l], -1)
                 code = jnp.where(l < depth_s[b], 4 * owner_s[b, l] + slot_s[b, l] + 1, 0)
-                table = jnp.where((lane == name) & (sub == 2 + b), slot_s[b, l] + 1, table)
                 table = jnp.where((lane == l) & (sub == b), code, table)
         tbuf[3] = table
 
     root_in.wait()
     prepare_root()
     node_in.wait()
-    prepare_nodes()
-    for copy in small_in:
-        copy.wait()
-    prepare_table()
-    q_in.wait()
+    prepare_nodes((0, 1), (0,))
 
     pl.semaphore_wait(bar, len(peers))
 
     def view(piece, pos, core):
         if piece < 2:
             return (rk, rv)[piece].at[pos, core]
-        for st, members in enumerate(STAGES):
-            if pos in members:
-                return nodes[piece // 2 - 1][piece % 2][st].at[members.index(pos), core]
+        return nodes[piece // 2 - 1][piece % 2].at[POS_DZ[pos] % ZN, core]
 
     started = []
 
@@ -177,34 +166,56 @@
             for piece in (2 * kind, 2 * kind + 1):
                 ccopy(piece, pos).wait_recv()
 
-    def qcopy(j):
+    def slot_dx(j):
+        return jnp.where(j == 0, 2, 2 * j - 1)
+
+    def slot_there(j):
+        return lax.rem(3 - j, 3)
+
+    def split(u):
+        return jnp.where(u < 6, lax.rem(u, 3), 3), jnp.where(u < 6, lax.div(u, 3), u - 6)
+
+    def qcopy(j, b):
+        there = (3 - j) % 3
         return pltpu.make_async_remote_copy(
-            qbuf.at[3], qbuf.at[2 - j], qsend.at[j], qrecv.at[2 - j], device_id=dev(dx=j + 1), device_id_type=MESH
+            qbuf.at[6 + b], qbuf.at[3 * b + there], qsend.at[j, b], qrecv.at[there, b],
+            device_id=dev(dx=SLOT_DX[j]), device_id_type=MESH,
         )
 
     def tcopy(j):
+        there = (3 - j) % 3
         return pltpu.make_async_remote_copy(
-            tbuf.at[3], tbuf.at[2 - j], tsend.at[j], trecv.at[2 - j], device_id=dev(dx=j + 1), device_id_type=MESH
+            tbuf.at[3], tbuf.at[there], tsend.at[j], trecv.at[there], device_id=dev(dx=SLOT_DX[j]), device_id_type=MESH
         )
 
     send_own(0, 0)
     send_own(0, 1)
     send_own(1, 0)
+    q_in.wait()
+    for j in (1, 2, 0):
+        for b in range(2):
+            go(qcopy(j, b))
+    for piece in range(4):
+        go(ccopy(piece, 0))
+    for copy in small_in:
+        copy.wait()
+    prepare_table()
     for j in range(3):
         go(tcopy(j))
-    for j in (0, 2, 1):
-        go(qcopy(j))
-    for piece in range(NPIECE):
-        go(ccopy(piece, 0))
-    own_in.wait()
-    prepare_own()
     hop(0, 0, 1)
     hop(0, 1, 1)
     send_own(1, 1)
+    prepare_nodes((), (1,))
+    go(ccopy(4, 0))
+    go(ccopy(5, 0))
+    own_in.wait()
+    prepare_own()
+    hop(0, 0, 2)
+    hop(0, 1, 2)
+    send_own(2, 0)
 
     def queries_of(u, h):
-        j, b = u // 2, u % 2
-        parts = [qbuf[j, b, :, h * 1024 + g * 128 : h * 1024 + g * 128 + 128] for g in range(GROUP)]
+        parts = [qbuf[u, :, h * 1024 + g * 128 : h * 1024 + g * 128 + 128] for g in range(GROUP)]
         return jnp.concatenate(parts, axis=0)
 
     def scores_of(keys, q):
@@ -232,21 +243,19 @@
             acc[6 + b, h] = jnp.dot(with_ones(ownv[b, h]), p, preferred_element_type=f32)
             md[6 + b, h] = jnp.broadcast_to(m, (8, ROWS))
 
-    hop(0, 0, 2)
-    hop(0, 1, 2)
-    send_own(2, 0)
     hop(0, 0, 3)
     hop(0, 1, 3)
     send_own(2, 1)
     hop(1, 0, 1)
     hop(1, 1, 1)
+    for j in range(3):
+        tcopy((3 - j) % 3).wait_recv()
+    t_in = local(9, tbuf, tsm)
+    hop(0, 0, 4)
     hop(2, 0, 1)
     for j in range(3):
-        tcopy(2 - j).wait_recv()
-    t_in = local(9, tbuf, tsm)
-    hop(0, 0, 4)
-    for j in (2, 0, 1):
-        qcopy(2 - j).wait_recv()
+        for b in range(2):
+            qcopy((3 - j) % 3, b).wait_recv()
     t_in.wait()
     settle(0, range(ZN))
     for h in range(2):
@@ -260,13 +269,12 @@
         q = queries_of(u, h)
         old = md[u, h, 0:1, :]
         top = old
-        s = scores_of(keys[0] if len(keys) == 1 else jnp.concatenate(keys, axis=0), q)
-        sbuf[t][0 : s.shape[0], :] = s
-        at = 0
-        for k, bias in zip(keys, biases):
-            best = jnp.max(s[at : at + k.shape[0]], axis=0, keepdims=True)
-            top = jnp.maximum(top, best if bias is None else best + bias)
-            at += k.shape[0]
+        for i in range(0, len(keys), 2):
+            s = scores_of(jnp.concatenate(keys[i : i + 2], axis=0), q)
+            sbuf[t][i * 128 : i * 128 + 256, :] = s
+            for n in range(2):
+                best = jnp.max(s[n * 128 : n * 128 + 128], axis=0, keepdims=True)
+                top = jnp.maximum(top, best if biases is None else best + biases[i + n])
         md[u, h, 0:1, :] = top
         rbuf[t][0:1, :] = top * C2
         rbuf[t][1:2, :] = jnp.exp2((old - top) * C2)
@@ -274,13 +282,10 @@
     def unit_b(u, h, t, vts, biases):
         low, factor = rbuf[t][0:1, :], rbuf[t][1:2, :]
         weights = []
-        at = 0
-        for vt, bias in zip(vts, biases):
-            width = vt.shape[1]
-            less = low if bias is None else low - bias
-            weights.append(jnp.exp2(sbuf[t][at : at + width, :] * C2 - less).astype(bf16))
-            at += width
-        p = weights[0] if len(weights) == 1 else jnp.concatenate(weights, axis=0)
+        for i in range(8):
+            less = low if biases is None else low - biases[i]
+            weights.append(jnp.exp2(sbuf[t][i * 128 : i * 128 + 128, :] * C2 - less).astype(bf16))
+        p = jnp.concatenate(weights, axis=0)
         vt = vts[0] if len(vts) == 1 else jnp.concatenate(vts, axis=1)
         acc[u, h] = acc[u, h] * factor + jnp.dot(with_ones(vt), p, preferred_element_type=f32)
 
@@ -310,57 +315,37 @@
 
     def root_stage(h, hooks=()):
         def first(u, t):
-            unit_a(u, h, t, [jnp.concatenate([rk[p, core, h] for p in range(ZN) for core in range(2)], axis=0)], [None])
+            unit_a(u, h, t, [jnp.concatenate([rk[p, 0, h], rk[p, 1, h]], axis=0) for p in range(ZN)], None)
 
         def second(u, t):
-            unit_b(u, h, t, [rvt[h]], [None])
+            unit_b(u, h, t, [rvt[h]], None)
 
         pipeline(first, second, None, hooks)
 
     def bias_of(active):
         return jnp.where(active, 0.0, NEG).astype(f32)
 
-    def near_stage(h, hooks=()):
+    def node_stage(h, after=None, hooks=()):
         def names(u):
+            j, b = split(u)
             got, biases = [], []
             for l in range(8):
-                code = tsm[u // 2, u % 2, l]
+                code = tsm[j, b, l]
                 owner = code >> 2
-                at = ((owner >> 3) - z + (2 + ZN)) & (ZN - 1)
+                at = ((owner >> 3) - z + ZN) & (ZN - 1)
                 core = (owner + c) & 1
-                mine = (code > 0) & (((owner >> 1) & (XN - 1)) == x) & (at < NEAR)
+                mine = (code > 0) & (((owner >> 1) & (XN - 1)) == x)
                 biases.append(bias_of(mine))
-                got.append((jnp.clip(at, 0, NEAR - 1), core, jnp.clip((code & 3) - 1, 0, SLOTS - 1)))
+                got.append((at, core, jnp.clip((code & 3) - 1, 0, SLOTS - 1)))
             return got, biases
 
         def first(u, t):
             at, biases = names(u)
-            unit_a(u, h, t, [nodes[h][0][0][a] for a in at], biases)
+            unit_a(u, h, t, [nodes[h][0][a] for a in at], biases)
 
         def second(u, t):
             at, biases = names(u)
-            unit_b(u, h, t, [nodes[h][1][0][a] for a in at], biases)
-
-        pipeline(first, second, None, hooks)
-
-    def far_stage(h, st, after=None, hooks=()):
-        members = [(i, pos, core) for i, pos in enumerate(STAGES[st]) for core in range(2)]
-
-        def names(u):
-            got = []
-            for i, pos, core in members:
-                zz = lax.rem(z + POS_DZ[pos] + ZN, ZN)
-                owner = zz * 8 + x * 2 + (c if core == 0 else 1 - c)
-                got.append(tsm[u // 2, 2 + u % 2, owner])
-            return [jnp.clip(g - 1, 0, SLOTS - 1) for g in got], [bias_of(g > 0) for g in got]
-
-        def first(u, t):
-            at, biases = names(u)
-            unit_a(u, h, t, [nodes[h][0][st][i, core, a] for (i, _, core), a in zip(members, at)], biases)
-
-        def second(u, t):
-            at, biases = names(u)
-            unit_b(u, h, t, [nodes[h][1][st][i, core, a] for (i, _, core), a in zip(members, at)], biases)
+            unit_b(u, h, t, [nodes[h][1][a] for a in at], biases)
 
         pipeline(first, second, after, hooks)
 
@@ -369,29 +354,28 @@
         b = (v - a).astype(bf16).astype(f32)
         return [a, b, v - a - b]
 
-    def ocopy(u, h):
-        j, b = u // 2, u % 2
+    def ocopy(j, b, h):
+        there = slot_there(j)
         return pltpu.make_async_remote_copy(
-            sendbuf.at[h, j, b], recvbuf.at[h, 2 - j, b], osend.at[h, j, b], orecv.at[h, 2 - j, b],
-            device_id=dev(dx=j + 1), device_id_type=MESH,
+            sendbuf.at[h, j, b], recvbuf.at[h, there, b], osend.at[h, j, b], orecv.at[h, there, b],
+            device_id=dev(dx=slot_dx(j)), device_id_type=MESH,
         )
 
     def send_part(h):
         def after(u):
-            j, b = u // 2, u % 2
+            j, b = split(u)
             sendbuf[h, j, b, :DIM, :] = acc[u, h, :DIM, :].astype(bf16)
             tail = three(md[u, h, 0:1, :]) + three(acc[u, h, DIM : DIM + 1, :])
             tail = jnp.concatenate(tail + [jnp.zeros((TAIL - 6, ROWS), f32)], axis=0)
             sendbuf[h, j, b, DIM:, :] = tail.astype(bf16)
-            ocopy(u, h).start()
+            ocopy(j, b, h).start()
 
         return after
 
     def merge(h):
-        for j in range(3):
-            for b in range(2):
-                ocopy(2 * (2 - j) + b, h).wait_recv()
         for b in range(2):
+            for j in range(3):
+                ocopy((3 - j) % 3, b, h).wait_recv()
             tops, dens, sums = [md[6 + b, h, 0:1, :]], [acc[6 + b, h, DIM : DIM + 1, :]], [acc[6 + b, h, :DIM, :]]
             for j in range(3):
                 tail = recvbuf[h, j, b, DIM:, :].astype(f32)
@@ -413,28 +397,19 @@
                 att[b, :, at : at + 128] = rows[g * SEG : g * SEG + SEG, :]
 
     root_stage(0)
-    hop(1, 0, 2)
-    root_stage(1, [(1, lambda: hop(1, 1, 2))])
-    settle(1, (0, 1, 2, 3, 4))
-
-    def hook_a():
-        hop(1, 0, 3)
-        hop(2, 1, 1)
-
-    near_stage(0, [(1, hook_a)])
+    root_stage(1, [(1, lambda: hop(1, 0, 2)), (2, lambda: hop(1, 1, 2))])
+    hop(1, 0, 3)
+    hop(2, 1, 1)
+    hop(2, 0, 2)
     hop(1, 1, 3)
-    settle(1, (5, 6))
-    far_stage(0, 1, None, [(1, lambda: hop(2, 0, 2))])
     hop(1, 0, 4)
-    settle(1, (7,))
-    far_stage(0, 2, send_part(0))
     hop(2, 1, 2)
-    settle(2, (0, 1, 2, 3, 4))
-    near_stage(1, [(1, lambda: hop(2, 0, 3)), (2, lambda: hop(2, 1, 3))])
-    settle(2, (5, 6))
-    far_stage(1, 1, None, [(1, lambda: hop(2, 0, 4))])
-    settle(2, (7,))
-    far_stage(1, 2, send_part(1))
+    settle(1, range(ZN))
+    node_stage(0, send_part(0), [(2, lambda: hop(2, 0, 3))])
+    hop(2, 1, 3)
+    hop(2, 0, 4)
+    settle(2, range(ZN))
+    node_stage(1, send_part(1))
     merge(0)
     merge(1)
 
@@ -460,8 +435,9 @@
     for copy in started:
         copy.wait_send()
     for h in range(2):
-        for u in range(6):
-            ocopy(u, h).wait_send()
+        for j in range(3):
+            for b in range(2):
+                ocopy(j, b, h).wait_send()
 
 
 def on_device(queries, root_kv, node_kv, own_kv, anc_owner, anc_slot, depth_len, seg_len, norm_gain):
@@ -474,9 +450,7 @@
         kv = kv.transpose(tuple(range(n)) + (n + 1, n, n + 2))
         return kv.reshape(-1, DIM)
 
-    node_refs = [
-        pltpu.VMEM((len(members), 2, SLOTS, 128, 128), bf16) for _ in range(4) for members in STAGES
-    ]
+    node_refs = [pltpu.VMEM((ZN, 2, SLOTS, 128, 128), bf16) for _ in range(4)]
     dma = pltpu.SemaphoreType.DMA
     scratch = [
         pltpu.VMEM((2 * 2 * ROOT, DIM), bf16),
@@ -487,7 +461,7 @@
         pltpu.SMEM((2,), jnp.int32),
         pltpu.SMEM((2,), jnp.int32),
         pltpu.VMEM((2048,), bf16),
-        pltpu.VMEM((XN, 2, SEG, 2048), bf16),
+        pltpu.VMEM((2 * XN, SEG, 2048), bf16),
         pltpu.VMEM((ZN, 2, 2, ROOT, DIM), bf16),
         pltpu.VMEM((ZN, 2, 2, ROOT, DIM), bf16),
         pltpu.VMEM((2, DIM, ZN * 2 * ROOT), bf16),
@@ -511,8 +485,8 @@
         dma((NPIECE, 2, 4)),
         dma((NPIECE, 8)),
         dma((NPIECE, 8)),
-        dma((3,)),
-        dma((3,)),
+        dma((3, 2)),
+        dma((3, 2)),
         dma((3,)),
         dma((3,)),
         dma((2, 3, 2)),

time: 68.7 us -> 66.9 us (0.974)
  Pallas kernels: 66.6 us -> 64.2 us
    pallas_call x1, Pallas kernels: 66.6 us -> 64.2 us  [on_device(): pl.pallas_call(kernel, out_shape=jax.ShapeDtypeStruct(queries.shape, bf16...]
where the time goes in v3:
time: 66.9 us; the launch traced here: 65.9 us
  Pallas kernels  64.2 us (96%)
  local copies, waits for them, and re-layouts  1.67 us (2%)
    pallas_call x1, Pallas kernels, on_device(): pl.pallas_call(kernel, out_shape=jax.ShapeDtypeStruct(queries.shape, bf16...  64.2 us
    unnamed x1, local copies, waits for them, and re-layouts  1.67 us

profile of v3, /device:TPU:2, one launch (start us, length us, event | category | flops | bytes accessed | tf_op | source)
XLA Modules:
  0.0 65.9 jit_solution(10642088062264688811)
XLA Ops:
  0.0 64.2 %tree_attention.1 = bf16[2,32,2048]{2,1,0:T(8,128)(2,1)} custom-call(bf16[2,32,2048]{2,1,0:T(8,128)(2,1)} %q_hbm.1, bf16[256,128]{1,0:T(8,128)(2,1)} %bitcast.16, bf16[1536,128]{1,0:T(8,128)(2,1)} %bitcast.15, bf16[256,128]{1,0:T(8,128)(2,1)} %bitcast.17, s32[2,8]{1,0:T(2,128)} %owner_hbm.1, s32[2,8]{1,0:T(2,128)} %slot_hbm.1, s32[2]{0:T(128)} %depth_hbm.1, ...), custom_call_target="tpu_custom_call" | custom-call | tf_op jit(solution)/shard_map/tree_attention/pallas_call | solution.py:498
  64.2 1.7 %copy.14 = bf16[2,32,2048]{2,1,0:T(8,128)(2,1)} copy(bf16[2,32,2048]{2,1,0:T(8,128)(2,1)} %tree_attention.1) | data formatting | bytes 524288

commit v4 on v3

--- a/solution.py
+++ b/solution.py
@@ -119,9 +119,6 @@
 
     root_in.wait()
     prepare_root()
-    node_in.wait()
-    prepare_nodes((0, 1), (0,))
-
     pl.semaphore_wait(bar, len(peers))
 
     def view(piece, pos, core):
@@ -190,6 +187,8 @@
 
     send_own(0, 0)
     send_own(0, 1)
+    node_in.wait()
+    prepare_nodes((0, 1), (0,))
     send_own(1, 0)
     q_in.wait()
     for j in (1, 2, 0):
@@ -502,12 +501,17 @@
         out_specs=pl.BlockSpec(memory_space=pltpu.VMEM),
         scratch_shapes=scratch,
         compiler_params=pltpu.CompilerParams(
-            collective_id=0, has_side_effects=True, vmem_limit_bytes=64 * 2**20
+            collective_id=0, has_side_effects=True, vmem_limit_bytes=48 * 2**20
         ),
         name="tree_attention",
     )(
-        queries, rows_of(root_kv), rows_of(node_kv), rows_of(own_kv),
-        anc_owner, anc_slot, depth_len, seg_len, norm_gain,
+        *[
+            pltpu.with_memory_space_constraint(v, pltpu.HBM)
+            for v in (
+                queries, rows_of(root_kv), rows_of(node_kv), rows_of(own_kv),
+                anc_owner, anc_slot, depth_len, seg_len, norm_gain,
+            )
+        ]
     )
 
 

time: 66.9 us -> 64.9 us (0.970)
  local copies, waits for them, and re-layouts: 1.67 us -> 0.71 us
  Pallas kernels: 64.2 us -> 63.5 us
    unnamed x1, local copies, waits for them, and re-layouts: 1.67 us -> 0.71 us
    pallas_call x1, Pallas kernels: 64.2 us -> 63.5 us  [on_device(): pl.pallas_call(kernel, out_shape=jax.ShapeDtypeStruct(queries.shape, bf16...]
where the time goes in v4:
time: 64.9 us; the launch traced here: 64.2 us
  Pallas kernels  63.5 us (98%)
  local copies, waits for them, and re-layouts  0.71 us (1%)
    pallas_call x1, Pallas kernels, on_device(): pl.pallas_call(kernel, out_shape=jax.ShapeDtypeStruct(queries.shape, bf16...  63.5 us

profile of v4, /device:TPU:2, one launch (start us, length us, event | category | flops | bytes accessed | tf_op | source)
XLA Modules:
  0.0 64.2 jit_solution(14893623707999015667)
XLA Ops:
  0.0 63.5 %tree_attention.1 = bf16[2,32,2048]{2,1,0:T(8,128)(2,1)S(1)} custom-call(bf16[2,32,2048]{2,1,0:T(8,128)(2,1)} %q_hbm.1, bf16[256,128]{1,0:T(8,128)(2,1)} %bitcast.16, bf16[1536,128]{1,0:T(8,128)(2,1)} %bitcast.15, bf16[256,128]{1,0:T(8,128)(2,1)} %bitcast.17, s32[2,8]{1,0:T(2,128)} %owner_hbm.1, s32[2,8]{1,0:T(2,128)} %slot_hbm.1, s32[2]{0:T(128)} %depth_hbm.1, ...), custom_call_target="tpu_custom_call" | custom-call | tf_op jit(solution)/shard_map/tree_attention/pallas_call | solution.py:497
  63.5 0.7 %copy.14 = bf16[2,32,2048]{2,1,0:T(8,128)(2,1)} copy(bf16[2,32,2048]{2,1,0:T(8,128)(2,1)S(1)} %tree_attention.1) | data formatting | bytes 524288

commit v5 on v4

v5 whole, which is shorter than its diff:
```python
import functools
import math

import jax
import jax.numpy as jnp
from jax import lax
from jax.experimental import pallas as pl
from jax.experimental.pallas import tpu as pltpu
from jax.sharding import PartitionSpec as P

MESH = pl.DeviceIdType.MESH
HEADS = 64
DIM = 128
SEG = 32
GROUP = 8
SLOTS = 3
ROWS = GROUP * SEG
ROOT = 64
ZN = 8
XN = 4
C2 = math.log2(math.e) / math.sqrt(DIM)
NEG = -1e30
TAIL = 16
POS_DZ = (0, -1, 1, -2, 2, -3, 3, 4)
SLOT_DX = (2, 1, 3)
NRING = 6


def pos_of(step, direction):
    return 7 if step == 4 else 2 * step - 1 + direction


def kernel(
    q_hbm, root_hbm, node_hbm, own_hbm, owner_hbm, slot_hbm, depth_hbm, seg_hbm, gain_hbm, out_ref,
    root_x, node_x, own_x, owner_s, slot_s, depth_s, seg_s, gain_ref,
    qb0, qb1, rk0, rv0, rvt0, rk1, rv1, rvt1, ownk, ownv, k0, v0, k1, v1,
    acc0, acc1, md0, md1, s0, s1, r0, r1, tx, tz, txs, tzs, send0, recv0, send1, recv1, att, ssq, ssq_in,
    zsend, zrecv, csend, crecv, xsend, xrecv, dsend, drecv, qsend, qrecv, tsend, trecv, usend, urecv,
    osend, orecv, psend, precv, ysend, yrecv, lsem,
):
    bf16, f32 = jnp.bfloat16, jnp.float32
    y = lax.axis_index("blk")
    r = lax.axis_index("branch")
    z, x, c = r // 8, (r // 2) % 4, r % 2

    def dev(dy=0, dz=0, dx=0, dc=0):
        zz = lax.rem(z + dz + ZN, ZN)
        xx = lax.rem(x + dx + XN, XN)
        cc = lax.rem(c + dc, 2)
        return (lax.rem(y + dy, 4), zz * 8 + xx * 2 + cc)

    def remote(src, dst, ssem, rsem, to):
        return pltpu.make_async_remote_copy(src, dst, ssem, rsem, device_id=to, device_id_type=MESH)

    bar = pltpu.get_barrier_semaphore()
    up, down, other = dev(dz=1), dev(dz=-1), dev(dc=1)
    peers = [other] + [dev(dz=d) for d in range(1, 8)]
    peers += [dev(dx=d) for d in (1, 2, 3)] + [dev(dy=d) for d in (1, 2, 3)]
    for p in peers:
        pl.semaphore_signal(bar, inc=1, device_id=p, device_id_type=MESH)

    def local(i, src, dst):
        copy = pltpu.make_async_copy(src, dst, lsem.at[i])
        copy.start()
        return copy

    root_in = local(1, root_hbm, root_x)
    node_in = local(0, node_hbm, node_x)
    small_in = [
        local(2, owner_hbm, owner_s), local(3, slot_hbm, slot_s), local(4, depth_hbm, depth_s), local(5, seg_hbm, seg_s)
    ]
    q_in = [
        local(6, q_hbm.at[:, :, pl.ds(0, 1024)], qb0.at[pl.ds(6, 2)]),
        local(9, q_hbm.at[:, :, pl.ds(1024, 1024)], qb1.at[pl.ds(0, 2)]),
    ]
    own_in = local(7, own_hbm, own_x)
    gain_in = local(8, gain_hbm, gain_ref)

    row = lax.broadcasted_iota(jnp.int32, (128, 128), 0)
    col = lax.broadcasted_iota(jnp.int32, (128, 128), 1)
    want = (row % 32) * 4 + row // 32
    pick = jnp.where(col == want, 1.0, 0.0).astype(bf16)

    def apart(ref, first):
        return jnp.dot(pick, ref[first : first + 128, :], preferred_element_type=f32)

    def prepare_root():
        got = [apart(root_x, t * 128).astype(bf16) for t in range(2)]
        for h, (kr, vr) in enumerate(((rk0, rv0), (rk1, rv1))):
            for t in range(2):
                kr[0, 0, t * 32 : t * 32 + 32, :] = got[t][h * 64 : h * 64 + 32]
                vr[0, 0, t * 32 : t * 32 + 32, :] = got[t][h * 64 + 32 : h * 64 + 64]

    def prepare_nodes(h, kr, vr):
        for s in range(SLOTS):
            got = [apart(node_x, (s * 4 + t) * 128) for t in range(4)]
            keys = jnp.concatenate([g[h * 64 : h * 64 + 32] for g in got], axis=0)
            vals = jnp.concatenate([g[h * 64 + 32 : h * 64 + 64] for g in got], axis=0)
            kr[0, 0, s] = keys.astype(bf16)
            vr[0, 0, s] = jnp.transpose(vals).astype(bf16)

    def prepare_own():
        zeros96 = jnp.zeros((96, 128), f32)
        for b in range(2):
            got = apart(own_x, b * 128)
            for h in range(2):
                keys = jnp.concatenate([got[h * 64 : h * 64 + 32], zeros96], axis=0)
                vals = jnp.concatenate([got[h * 64 + 32 : h * 64 + 64], zeros96], axis=0)
                ownk[b, h] = keys.astype(bf16)
                ownv[b, h] = jnp.transpose(vals).astype(bf16)

    def prepare_table():
        lane = lax.broadcasted_iota(jnp.int32, (8, 128), 1)
        sub = lax.broadcasted_iota(jnp.int32, (8, 128), 0)
        table = jnp.zeros((8, 128), jnp.int32)
        for b in range(2):
            for l in range(8):
                code = jnp.where(l < depth_s[b], 4 * owner_s[b, l] + slot_s[b, l] + 1, 0)
                table = jnp.where((lane == l) & (sub == b), code, table)
        tx[3] = table
        tz[0] = table

    root_in.wait()
    prepare_root()
    pl.semaphore_wait(bar, len(peers))

    started = []

    def go(copy):
        copy.start()
        started.append(copy)

    def view(piece, pos, core):
        dz = POS_DZ[pos] % ZN
        if piece < 2:
            return qb1.at[2 * dz + piece]
        return (k0, v0, rk0, rv0)[piece - 2].at[dz, core]

    def zcopy(piece, direction, step):
        if step > 1:
            src = view(piece, pos_of(step - 1, direction), 0)
        elif piece < 2:
            src = q_hbm.at[piece, :, pl.ds(1024, 1024)]
        else:
            src = view(piece, 0, 0)
        return remote(
            src, view(piece, pos_of(step, direction), 0), zsend.at[piece, direction, step - 1],
            zrecv.at[piece, direction, step - 1], up if direction == 0 else down,
        )

    def ccopy(piece, pos):
        return remote(view(piece, pos, 0), view(piece, pos, 1), csend.at[piece, pos], crecv.at[piece, pos], other)

    def send_own(kind, which):
        for direction in (0, 1):
            go(zcopy(2 * kind + (which ^ direction), direction, 1))

    def hop(kind, which, step):
        for direction in (0, 1):
            piece = 2 * kind + (which ^ direction)
            zcopy(piece, direction, step).wait_recv()
            if step < 3 or (step == 3 and which == 0):
                go(zcopy(piece, direction, step + 1))
            if kind > 0:
                go(ccopy(piece, pos_of(step, direction)))

    def settle(kind):
        for pos in range(ZN):
            for piece in (2 * kind, 2 * kind + 1):
                ccopy(piece, pos).wait_recv()

    xrefs = (k1, v1, rk1, rv1)

    def xcopy(piece, dx):
        there = 4 - dx
        return remote(
            xrefs[piece].at[0, 0], xrefs[piece].at[there, 0], xsend.at[piece, dx - 1], xrecv.at[piece, there - 1], dev(dx=dx)
        )

    def dcopy(piece, rel):
        ref = xrefs[piece]
        return remote(ref.at[rel, 0], ref.at[rel, 1], dsend.at[piece, rel], drecv.at[piece, rel], other)

    def slot_dx(j):
        return jnp.where(j == 0, 2, 2 * j - 1)

    def slot_there(j):
        return lax.rem(3 - j, 3)

    def split(u):
        return jnp.where(u < 6, lax.rem(u, 3), 3), jnp.where(u < 6, lax.div(u, 3), u - 6)

    def qcopy(j, b):
        there = (3 - j) % 3
        return remote(
            q_hbm.at[b, :, pl.ds(0, 1024)], qb0.at[3 * b + there], qsend.at[j, b], qrecv.at[there, b], dev(dx=SLOT_DX[j])
        )

    def tcopy(j):
        there = (3 - j) % 3
        return remote(tx.at[3], tx.at[there], tsend.at[j], trecv.at[there], dev(dx=SLOT_DX[j]))

    def ucopy(dz):
        return remote(tz.at[0], tz.at[8 - dz], usend.at[dz - 1], urecv.at[7 - dz], dev(dz=dz))

    send_own(0, 0)
    send_own(0, 1)
    send_own(2, 0)
    send_own(2, 1)
    node_in.wait()
    prepare_nodes(1, k1, v1)
    for piece in (0, 1):
        for dx in (1, 3, 2):
            go(xcopy(piece, dx))
    hop(0, 0, 1)
    hop(0, 1, 1)
    prepare_nodes(0, k0, v0)
    send_own(1, 0)
    for piece in (2, 3):
        for dx in (1, 3, 2):
            go(xcopy(piece, dx))
    for copy in small_in:
        copy.wait()
    prepare_table()
    for dz in range(1, 8):
        go(ucopy(dz))
    hop(0, 0, 2)
    hop(0, 1, 2)
    for j in range(3):
        go(tcopy(j))
    for b in range(2):
        for j in (1, 2, 0):
            go(qcopy(j, b))
    for piece in range(4):
        go(dcopy(piece, 0))
        go(ccopy(2 + piece, 0))
    own_in.wait()
    prepare_own()
    hop(0, 0, 3)
    send_own(1, 1)
    hop(2, 0, 1)
    hop(2, 1, 1)
    hop(1, 0, 1)
    for copy in q_in:
        copy.wait()

    qbs, accs, mds = (qb0, qb1), (acc0, acc1), (md0, md1)

    def queries_of(u, h):
        return jnp.concatenate([qbs[h][u, :, g * 128 : g * 128 + 128] for g in range(GROUP)], axis=0)

    def scores_of(keys, q):
        return lax.dot_general(keys, q, (((1,), (1,)), ((), ())), preferred_element_type=f32)

    def with_ones(vt):
        return jnp.concatenate([vt, jnp.ones((TAIL, vt.shape[1]), bf16)], axis=0)

    def clear(h):
        def body(u, _):
            accs[h][u] = jnp.zeros((DIM + TAIL, ROWS), f32)
            mds[h][u] = jnp.full((8, ROWS), NEG, f32)
            return 0

        return body

    lax.fori_loop(0, 6, clear(0), 0)
    lax.fori_loop(2, 16, clear(1), 0)
    for piece in (0, 1, 2, 3):
        for dx in (1, 3, 2):
            xcopy(piece, dx).wait_recv()
            go(dcopy(piece, 4 - dx))
    hop(0, 1, 3)
    key_at = lax.broadcasted_iota(jnp.int32, (128, ROWS), 0)
    query_at = lax.rem(lax.broadcasted_iota(jnp.int32, (128, ROWS), 1), SEG)
    causal = key_at <= query_at
    for b in range(2):
        for h in range(2):
            u = (6 + b, b)[h]
            s = scores_of(ownk[b, h], queries_of(u, h))
            s = jnp.where(causal, s, NEG)
            m = jnp.max(s, axis=0, keepdims=True)
            p = jnp.exp2(s * C2 - m * C2).astype(bf16)
            accs[h][u] = jnp.dot(with_ones(ownv[b, h]), p, preferred_element_type=f32)
            mds[h][u] = jnp.broadcast_to(m, (8, ROWS))
    for dz in range(1, 8):
        ucopy(dz).wait_recv()
    for j in range(3):
        tcopy((3 - j) % 3).wait_recv()
    t_in = [local(10, tx, txs), local(11, tz, tzs)]
    hop(0, 0, 4)
    for copy in t_in:
        copy.wait()
    for piece in range(4):
        for rel in range(4):
            dcopy(piece, rel).wait_recv()

    def turn(vr, vt, n):
        for p in range(n):
            pair = jnp.concatenate([vr[p, 0], vr[p, 1]], axis=0).astype(f32)
            vt[p] = jnp.transpose(pair).astype(bf16)

    turn(rv1, rvt1, 4)

    sbuf, rbuf = (s0, s1), (r0, r1)

    def unit_a(u, h, t, keys, biases):
        q = queries_of(u, h)
        old = mds[h][u, 0:1, :]
        top = old
        for i in range(0, len(keys), 2):
            s = scores_of(jnp.concatenate(keys[i : i + 2], axis=0), q)
            sbuf[t][i * 128 : i * 128 + 256, :] = s
            for n in range(2):
                best = jnp.max(s[n * 128 : n * 128 + 128], axis=0, keepdims=True)
                top = jnp.maximum(top, best if biases[i + n] is None else best + biases[i + n])
        mds[h][u, 0:1, :] = top
        rbuf[t][0:1, :] = top * C2
        rbuf[t][1:2, :] = jnp.exp2((old - top) * C2)

    def unit_b(u, h, t, vts, biases):
        low, factor = rbuf[t][0:1, :], rbuf[t][1:2, :]
        weights = []
        for i, bias in enumerate(biases):
            less = low if bias is None else low - bias
            weights.append(jnp.exp2(sbuf[t][i * 128 : i * 128 + 128, :] * C2 - less).astype(bf16))
        p = jnp.concatenate(weights, axis=0)
        vt = jnp.concatenate(vts, axis=1)
        accs[h][u] = accs[h][u] * factor + jnp.dot(with_ones(vt), p, preferred_element_type=f32)

    def pipeline(count, unit_1, unit_2, after=None, hooks=()):
        unit_1(0, 0)

        def body(j, _):
            unit_1(2 * j + 1, 1)
            unit_2(2 * j, 0)
            if after is not None:
                after(2 * j)
            unit_1(2 * j + 2, 0)
            unit_2(2 * j + 1, 1)
            if after is not None:
                after(2 * j + 1)
            return 0

        at = 0
        for when, hook in hooks:
            lax.fori_loop(at, when, body, 0)
            hook()
            at = when
        lax.fori_loop(at, count // 2 - 1, body, 0)
        unit_1(count - 1, 1)
        unit_2(count - 2, 0)
        unit_2(count - 1, 1)

    def bias_of(active):
        return jnp.where(active, 0.0, NEG).astype(f32)

    def pairs(ref, n):
        return [jnp.concatenate([ref[p, 0], ref[p, 1]], axis=0) for p in range(n)]

    def slot_of(code):
        return jnp.clip((code & 3) - 1, 0, SLOTS - 1)

    def column_stage(after, hooks=()):
        def names(u):
            j, b = split(u)
            got, biases = [], [None] * ZN
            for l in range(8):
                code = txs[j, b, l]
                owner = code >> 2
                biases.append(bias_of((code > 0) & (((owner >> 1) & (XN - 1)) == x)))
                got.append((((owner >> 3) - z + ZN) & (ZN - 1), (owner + c) & 1, slot_of(code)))
            return got, biases

        def first(u, t):
            at, biases = names(u)
            unit_a(u, 0, t, pairs(rk0, ZN) + [k0[a] for a in at], biases)

        def second(u, t):
            at, biases = names(u)
            unit_b(u, 0, t, [rvt0[p] for p in range(ZN)] + [v0[a] for a in at], biases)

        pipeline(8, first, second, after, hooks)

    def row_stage(hooks=()):
        def names(u):
            got, biases = [], [None] * XN
            for l in range(8):
                code = tzs[u // 2, u % 2, l]
                owner = code >> 2
                biases.append(bias_of((code > 0) & ((owner >> 3) == z)))
                got.append((((owner >> 1) - x + XN) & (XN - 1), (owner + c) & 1, slot_of(code)))
            return got, biases

        def first(u, t):
            at, biases = names(u)
            unit_a(u, 1, t, pairs(rk1, XN) + [k1[a] for a in at], biases)

        def second(u, t):
            at, biases = names(u)
            unit_b(u, 1, t, [rvt1[p] for p in range(XN)] + [v1[a] for a in at], biases)

        pipeline(16, first, second, None, hooks)

    def three(v):
        a = v.astype(bf16).astype(f32)
        b = (v - a).astype(bf16).astype(f32)
        return [a, b, v - a - b]

    def write(ref, total, top, den):
        ref[:DIM, :] = total.astype(bf16)
        tail = jnp.concatenate(three(top) + three(den) + [jnp.zeros((TAIL - 6, ROWS), f32)], axis=0)
        ref[DIM:, :] = tail.astype(bf16)

    def read(ref):
        tail = ref[DIM:, :].astype(f32)
        return ref[:DIM, :].astype(f32), tail[0:1] + tail[1:2] + tail[2:3], tail[3:4] + tail[4:5] + tail[5:6]

    def state(h, u):
        return accs[h][u, :DIM, :], mds[h][u, 0:1, :], accs[h][u, DIM : DIM + 1, :]

    def combine(parts):
        top = functools.reduce(jnp.maximum, [p[1] for p in parts])
        ws = [jnp.exp2((p[1] - top) * C2) for p in parts]
        return ws, top, sum(w * p[2] for w, p in zip(ws, parts))

    def ocopy(j, b):
        there = slot_there(j)
        return remote(send0.at[j, b], recv0.at[there, b], osend.at[j, b], orecv.at[there, b], dev(dx=slot_dx(j)))

    def send_part(u):
        j, b = split(u)
        write(send0.at[j, b], *state(0, u))
        ocopy(j, b).start()

    def pcopy(direction, step, b):
        return remote(
            send1.at[direction, step - 1, b], recv1.at[direction, step - 1, b], psend.at[direction, step - 1, b],
            precv.at[direction, step - 1, b], up if direction == 0 else down,
        )

    def pass_on(step, fresh):
        for direction in (0, 1):
            b = direction ^ fresh
            away = 5 - step if direction == 0 else 3 + step
            mine = state(1, 2 * away + b)
            if step > 2 or (step == 2 and fresh == 0):
                pcopy(direction, step - 1, b).wait_recv()
                parts = [mine, read(recv1.at[direction, step - 2, b])]
                ws, top, den = combine(parts)
                mine = (sum(w * p[0] for w, p in zip(ws, parts)), top, den)
            write(send1.at[direction, step - 1, b], *mine)
            go(pcopy(direction, step, b))

    def finish(h, b, u, parts):
        ws, top, den = combine(parts)
        inv = 1.0 / den
        total = sum(p[0] * (w * inv) for w, p in zip(ws, parts))
        live = lax.rem(lax.broadcasted_iota(jnp.int32, (1, ROWS), 1), SEG) < seg_s[b]
        total = jnp.where(live, total, 0.0)
        part = jnp.sum(total * total, axis=0, keepdims=True)
        ssq[b : b + 1, :] = part if h == 0 else ssq[b : b + 1, :] + part
        rows = jnp.transpose(total)
        for g in range(GROUP):
            at = h * 1024 + g * 128
            att[b, :, at : at + 128] = rows[g * SEG : g * SEG + SEG, :]

    def merge0(b):
        for j in range(3):
            ocopy((3 - j) % 3, b).wait_recv()
        finish(0, b, 6 + b, [state(0, 6 + b)] + [read(recv0.at[j, b]) for j in range(3)])

    def merge1(b):
        for direction in (0, 1):
            pcopy(direction, 4, b).wait_recv()
        finish(1, b, b, [state(1, b)] + [read(recv1.at[direction, 3, b]) for direction in (0, 1)])

    def hook_root():
        hop(2, 0, 2)
        hop(2, 1, 2)

    row_stage([(2, lambda: hop(1, 1, 1)), (3, hook_root), (5, lambda: hop(1, 0, 2))])
    hop(1, 1, 2)
    hop(2, 0, 3)
    hop(2, 1, 3)
    hop(1, 0, 3)
    pass_on(1, 0)
    pass_on(2, 1)
    hop(1, 1, 3)
    for j in range(3):
        for b in range(2):
            qcopy((3 - j) % 3, b).wait_recv()
    hop(2, 0, 4)
    settle(2)
    turn(rv0, rvt0, ZN)
    hop(1, 0, 4)
    pass_on(2, 0)
    settle(1)
    column_stage(send_part, [(1, lambda: pass_on(3, 1)), (2, lambda: pass_on(3, 0)), (3, lambda: pass_on(4, 1))])
    pass_on(4, 0)
    merge0(0)
    merge0(1)
    merge1(0)
    merge1(1)

    def ycopy(d):
        return pltpu.make_async_remote_copy(
            ssq, ssq_in.at[3 - d], ysend.at[d - 1], yrecv.at[3 - d], device_id=dev(dy=d), device_id_type=MESH
        )

    for d in (1, 2, 3):
        go(ycopy(d))
    for d in (1, 2, 3):
        ycopy(d).wait_recv()
    gain_in.wait()
    squares = jnp.transpose(ssq[...] + ssq_in[0] + ssq_in[1] + ssq_in[2])
    squares = sum(squares[g * SEG : g * SEG + SEG, :] for g in range(GROUP))
    scales = lax.rsqrt(squares / (HEADS * DIM) + 1e-6)
    for b in range(2):
        scale = scales[:, b : b + 1]
        for g in range(2 * GROUP):
            at = slice(g * 128, g * 128 + 128)
            out_ref[b, :, at] = (att[b, :, at] * scale * gain_ref[at].astype(f32).reshape(1, DIM)).astype(bf16)

    for copy in started:
        copy.wait_send()
    for j in range(3):
        for b in range(2):
            ocopy(j, b).wait_send()


def on_device(queries, root_kv, node_kv, own_kv, anc_owner, anc_slot, depth_len, seg_len, norm_gain):
    bf16, f32 = jnp.bfloat16, jnp.float32

    def rows_of(kv):
        lead = kv.shape[:-2]
        n = len(lead)
        kv = kv.reshape(lead + (2, 2, DIM))
        kv = kv.transpose(tuple(range(n)) + (n + 1, n, n + 2))
        return kv.reshape(-1, DIM)

    dma = pltpu.SemaphoreType.DMA
    scratch = [
        pltpu.VMEM((2 * 2 * ROOT, DIM), bf16),
        pltpu.VMEM((SLOTS * 2 * 2 * 128, DIM), bf16),
        pltpu.VMEM((2 * 2 * 2 * SEG, DIM), bf16),
        pltpu.SMEM((2, 8), jnp.int32),
        pltpu.SMEM((2, 8), jnp.int32),
        pltpu.SMEM((2,), jnp.int32),
        pltpu.SMEM((2,), jnp.int32),
        pltpu.VMEM((2048,), bf16),
        pltpu.VMEM((8, SEG, 1024), bf16),
        pltpu.VMEM((16, SEG, 1024), bf16),
        pltpu.VMEM((ZN, 2, ROOT, DIM), bf16),
        pltpu.VMEM((ZN, 2, ROOT, DIM), bf16),
        pltpu.VMEM((ZN, DIM, 2 * ROOT), bf16),
        pltpu.VMEM((XN, 2, ROOT, DIM), bf16),
        pltpu.VMEM((XN, 2, ROOT, DIM), bf16),
        pltpu.VMEM((XN, DIM, 2 * ROOT), bf16),
        pltpu.VMEM((2, 2, 128, DIM), bf16),
        pltpu.VMEM((2, 2, DIM, 128), bf16),
        pltpu.VMEM((ZN, 2, SLOTS, 128, DIM), bf16),
        pltpu.VMEM((ZN, 2, SLOTS, DIM, 128), bf16),
        pltpu.VMEM((XN, 2, SLOTS, 128, DIM), bf16),
        pltpu.VMEM((XN, 2, SLOTS, DIM, 128), bf16),
        pltpu.VMEM((8, DIM + TAIL, ROWS), f32),
        pltpu.VMEM((16, DIM + TAIL, ROWS), f32),
        pltpu.VMEM((8, 8, ROWS), f32),
        pltpu.VMEM((16, 8, ROWS), f32),
        pltpu.VMEM((2048, ROWS), f32),
        pltpu.VMEM((2048, ROWS), f32),
        pltpu.VMEM((8, ROWS), f32),
        pltpu.VMEM((8, ROWS), f32),
        pltpu.VMEM((XN, 8, 128), jnp.int32),
        pltpu.VMEM((ZN, 8, 128), jnp.int32),
        pltpu.SMEM((XN, 8, 128), jnp.int32),
        pltpu.SMEM((ZN, 8, 128), jnp.int32),
        pltpu.VMEM((3, 2, DIM + TAIL, ROWS), bf16),
        pltpu.VMEM((3, 2, DIM + TAIL, ROWS), bf16),
        pltpu.VMEM((2, 4, 2, DIM + TAIL, ROWS), bf16),
        pltpu.VMEM((2, 4, 2, DIM + TAIL, ROWS), bf16),
        pltpu.VMEM((2, SEG, 2048), f32),
        pltpu.VMEM((8, ROWS), f32),
        pltpu.VMEM((3, 8, ROWS), f32),
    ]
    for shape in ((NRING, 2, 4), (NRING, 8), (4, 3), (4, 4), (3, 2), (3,), (7,), (3, 2), (2, 4, 2), (3,)):
        scratch += [dma(shape), dma(shape)]
    scratch.append(dma((12,)))
    return pl.pallas_call(
        kernel,
        out_shape=jax.ShapeDtypeStruct(queries.shape, bf16),
        in_specs=[pl.BlockSpec(memory_space=pltpu.HBM)] * 9,
        out_specs=pl.BlockSpec(memory_space=pltpu.VMEM),
        scratch_shapes=scratch,
        compiler_params=pltpu.CompilerParams(
            collective_id=0, has_side_effects=True, vmem_limit_bytes=48 * 2**20
        ),
        name="tree_attention",
    )(
        *[
            pltpu.with_memory_space_constraint(v, pltpu.HBM)
            for v in (
                queries, rows_of(root_kv), rows_of(node_kv), rows_of(own_kv),
                anc_owner, anc_slot, depth_len, seg_len, norm_gain,
            )
        ]
    )


def solution(mesh):
    in_specs = (
        P("branch", None, "blk"),
        P("branch", None, "blk"),
        P("branch", None, None, "blk"),
        P("branch", None, None, "blk"),
        P("branch", None),
        P("branch", None),
        P("branch"),
        P("branch"),
        P("blk"),
    )
    return jax.shard_map(
        on_device, mesh=mesh, in_specs=in_specs, out_specs=P("branch", None, "blk"), check_vma=False
    )
```

time: 64.9 us -> 63.2 us (0.974)
  Pallas kernels: 63.5 us -> 62.2 us
    pallas_call x1, Pallas kernels: 63.5 us -> 62.2 us  [on_device(): pl.pallas_call(kernel, out_shape=jax.ShapeDtypeStruct(queries.shape, bf16...]
where the time goes in v5:
time: 63.2 us; the launch traced here: 62.9 us
  Pallas kernels  62.2 us (98%)
  local copies, waits for them, and re-layouts  0.71 us (1%)
    pallas_call x1, Pallas kernels, on_device(): pl.pallas_call(kernel, out_shape=jax.ShapeDtypeStruct(queries.shape, bf16...  62.2 us

profile of v5, /device:TPU:2, one launch (start us, length us, event | category | flops | bytes accessed | tf_op | source)
XLA Modules:
  0.0 62.9 jit_solution(2803016185422160719)
XLA Ops:
  0.0 62.2 %tree_attention.1 = bf16[2,32,2048]{2,1,0:T(8,128)(2,1)S(1)} custom-call(bf16[2,32,2048]{2,1,0:T(8,128)(2,1)} %q_hbm.1, bf16[256,128]{1,0:T(8,128)(2,1)} %bitcast.16, bf16[1536,128]{1,0:T(8,128)(2,1)} %bitcast.15, bf16[256,128]{1,0:T(8,128)(2,1)} %bitcast.17, s32[2,8]{1,0:T(2,128)} %owner_hbm.1, s32[2,8]{1,0:T(2,128)} %slot_hbm.1, s32[2]{0:T(128)} %depth_hbm.1, ...), custom_call_target="tpu_custom_call" | custom-call | tf_op jit(solution)/shard_map/tree_attention/pallas_call | solution.py:588
  62.2 0.7 %copy.14 = bf16[2,32,2048]{2,1,0:T(8,128)(2,1)} copy(bf16[2,32,2048]{2,1,0:T(8,128)(2,1)S(1)} %tree_attention.1) | data formatting | bytes 524288

commit v6 on v5

--- a/solution.py
+++ b/solution.py
@@ -459,10 +459,14 @@
         total = jnp.where(live, total, 0.0)
         part = jnp.sum(total * total, axis=0, keepdims=True)
         ssq[b : b + 1, :] = part if h == 0 else ssq[b : b + 1, :] + part
-        rows = jnp.transpose(total)
+        accs[h][u, :DIM, :] = total
+
+    def place(h, b, u):
+        rows = jnp.transpose(accs[h][u, :DIM, :])
         for g in range(GROUP):
             at = h * 1024 + g * 128
-            att[b, :, at : at + 128] = rows[g * SEG : g * SEG + SEG, :]
+            gain = gain_ref[at : at + 128].astype(f32).reshape(1, DIM)
+            att[b, :, at : at + 128] = rows[g * SEG : g * SEG + SEG, :] * gain
 
     def merge0(b):
         for j in range(3):
@@ -497,8 +501,11 @@
     settle(1)
     column_stage(send_part, [(1, lambda: pass_on(3, 1)), (2, lambda: pass_on(3, 0)), (3, lambda: pass_on(4, 1))])
     pass_on(4, 0)
-    merge0(0)
-    merge0(1)
+    gain_in.wait()
+    for b in range(2):
+        merge0(b)
+    for b in range(2):
+        place(0, b, 6 + b)
     merge1(0)
     merge1(1)
 
@@ -509,9 +516,10 @@
 
     for d in (1, 2, 3):
         go(ycopy(d))
+    for b in range(2):
+        place(1, b, b)
     for d in (1, 2, 3):
         ycopy(d).wait_recv()
-    gain_in.wait()
     squares = jnp.transpose(ssq[...] + ssq_in[0] + ssq_in[1] + ssq_in[2])
     squares = sum(squares[g * SEG : g * SEG + SEG, :] for g in range(GROUP))
     scales = lax.rsqrt(squares / (HEADS * DIM) + 1e-6)
@@ -519,7 +527,7 @@
         scale = scales[:, b : b + 1]
         for g in range(2 * GROUP):
             at = slice(g * 128, g * 128 + 128)
-            out_ref[b, :, at] = (att[b, :, at] * scale * gain_ref[at].astype(f32).reshape(1, DIM)).astype(bf16)
+            out_ref[b, :, at] = (att[b, :, at] * scale).astype(bf16)
 
     for copy in started:
         copy.wait_send()

time: 63.2 us -> 63.2 us (level)
  no operation moved by 1% of the time
where the time goes in v6:
time: 63.2 us; the launch traced here: 62.8 us
  Pallas kernels  62.1 us (98%)
  local copies, waits for them, and re-layouts  0.71 us (1%)
    pallas_call x1, Pallas kernels, on_device(): pl.pallas_call(kernel, out_shape=jax.ShapeDtypeStruct(queries.shape, bf16...  62.1 us

profile of v6, /device:TPU:2, one launch (start us, length us, event | category | flops | bytes accessed | tf_op | source)
XLA Modules:
  0.0 62.8 jit_solution(12220725136156339138)
XLA Ops:
  0.0 62.1 %tree_attention.1 = bf16[2,32,2048]{2,1,0:T(8,128)(2,1)S(1)} custom-call(bf16[2,32,2048]{2,1,0:T(8,128)(2,1)} %q_hbm.1, bf16[256,128]{1,0:T(8,128)(2,1)} %bitcast.16, bf16[1536,128]{1,0:T(8,128)(2,1)} %bitcast.15, bf16[256,128]{1,0:T(8,128)(2,1)} %bitcast.17, s32[2,8]{1,0:T(2,128)} %owner_hbm.1, s32[2,8]{1,0:T(2,128)} %slot_hbm.1, s32[2]{0:T(128)} %depth_hbm.1, ...), custom_call_target="tpu_custom_call" | custom-call | tf_op jit(solution)/shard_map/tree_attention/pallas_call | solution.py:596
  62.1 0.7 %copy.14 = bf16[2,32,2048]{2,1,0:T(8,128)(2,1)} copy(bf16[2,32,2048]{2,1,0:T(8,128)(2,1)S(1)} %tree_attention.1) | data formatting | bytes 524288

commit v7 on v6

--- a/solution.py
+++ b/solution.py
@@ -504,8 +504,6 @@
     gain_in.wait()
     for b in range(2):
         merge0(b)
-    for b in range(2):
-        place(0, b, 6 + b)
     merge1(0)
     merge1(1)
 
@@ -517,6 +515,7 @@
     for d in (1, 2, 3):
         go(ycopy(d))
     for b in range(2):
+        place(0, b, 6 + b)
         place(1, b, b)
     for d in (1, 2, 3):
         ycopy(d).wait_recv()

time: 63.2 us -> 63.1 us (level)
  no operation moved by 1% of the time
where the time goes in v7:
time: 63.1 us; the launch traced here: 62.8 us
  Pallas kernels  62.1 us (98%)
  local copies, waits for them, and re-layouts  0.71 us (1%)
    pallas_call x1, Pallas kernels, on_device(): pl.pallas_call(kernel, out_shape=jax.ShapeDtypeStruct(queries.shape, bf16...  62.1 us

profile of v7, /device:TPU:2, one launch (start us, length us, event | category | flops | bytes accessed | tf_op | source)
XLA Modules:
  0.0 62.8 jit_solution(17160765997495798091)
XLA Ops:
  0.0 62.1 %tree_attention.1 = bf16[2,32,2048]{2,1,0:T(8,128)(2,1)S(1)} custom-call(bf16[2,32,2048]{2,1,0:T(8,128)(2,1)} %q_hbm.1, bf16[256,128]{1,0:T(8,128)(2,1)} %bitcast.16, bf16[1536,128]{1,0:T(8,128)(2,1)} %bitcast.15, bf16[256,128]{1,0:T(8,128)(2,1)} %bitcast.17, s32[2,8]{1,0:T(2,128)} %owner_hbm.1, s32[2,8]{1,0:T(2,128)} %slot_hbm.1, s32[2]{0:T(128)} %depth_hbm.1, ...), custom_call_target="tpu_custom_call" | custom-call | tf_op jit(solution)/shard_map/tree_attention/pallas_call | solution.py:595
  62.1 0.7 %copy.14 = bf16[2,32,2048]{2,1,0:T(8,128)(2,1)} copy(bf16[2,32,2048]{2,1,0:T(8,128)(2,1)S(1)} %tree_attention.1) | data formatting | bytes 524288
